TPU v7x, 32 devices: a whole 2x2x4 slice. The times are simulated.
32 devices in a mesh: ctx: 8 (over y, x, core), tp: 4 (over z).
Axes of the slice: x: 2, y: 2, z: 4, core: 2. Of those that a mesh axis runs over, the one named last changes fastest.
Arguments:
- hidden: bfloat16 [8192, 8192], P('ctx', 'tp'), may hold values from -20 to 20
- norm_gain: bfloat16 [8192], P('tp'), may hold values from 0.5 to 1.5
- router_weight: bfloat16 [8192], P('tp'), may hold values from -0.0625 to 0.0625
- query_weight: bfloat16 [8192, 4096], P('tp'), may hold values from -29 to 29
- key_value_weight: bfloat16 [2, 8192, 512], P(None, 'tp'), may hold values from -1 to 1
- out_weight: bfloat16 [4096, 8192], P(None, 'tp'), may hold values from -0.5 to 0.5
- kept_rows: int32 [8, 512], replicated, may hold values from 0 to 1024, as said below
Outputs:
- block_update: bfloat16 [8192, 8192], P('ctx', 'tp')
Inputs may be any that keep to these rules, and one draw needn't show every extreme that they name: `kept_rows`: row c lists, in rising order, the distinct local indices of the kept rows of context shard c, then 1024 in every unused slot. The counts of kept rows over all shards sum to 2048; every shard keeps at least one row and some shard keeps exactly 512.
All inputs are finite; a program needn't handle non-finite values.
Results may differ from a plain program's by a relative error of at most 0.025.
Values may be sent and summed in bfloat16 or wider, within the bound.
A program may use at most 128 MiB of HBM per device.

v0:
```python
import jax
import jax.numpy as jnp
from jax import lax
from jax.sharding import PartitionSpec as P

D = 8192
H = 32
KVH = 4
HD = 128


EPSILON = 1e-05
MASKED_SCORE = -1e30


def shards(hidden, norm_gain, router_weight, query_weight, key_value_weight, out_weight, kept_rows):
    shard_index = lax.axis_index("ctx")
    tp_index = lax.axis_index("tp")
    ctx_count = lax.axis_size("ctx")
    tp_count = lax.axis_size("tp")
    token_count, width_local = hidden.shape
    capacity = kept_rows.shape[1]
    heads_local = H // tp_count
    own_rows = lax.dynamic_index_in_dim(kept_rows, shard_index, 0, keepdims=False)
    is_valid = own_rows < token_count
    safe_rows = jnp.minimum(own_rows, token_count - 1)
    kept_states = hidden[safe_rows]
    widened = kept_states.astype(jnp.float32)
    square_part = jnp.sum(widened * widened, axis=1)
    router_part = jnp.dot(kept_states, router_weight, preferred_element_type=jnp.float32)
    normed = (widened * norm_gain.astype(jnp.float32)).astype(jnp.bfloat16)
    square_sum, router_logit = lax.psum((square_part, router_part), "tp")
    inverse_rms = lax.rsqrt(square_sum / D + EPSILON)
    key_terms = lax.dot_general(
        key_value_weight, normed, (((1,), (1,)), ((), ())), preferred_element_type=jnp.float32
    )
    key_group = tp_index * heads_local // (H // KVH)
    query_sum = lax.psum_scatter(
        lax.dot_general(
            query_weight, normed, (((0,), (1,)), ((), ())), preferred_element_type=jnp.float32
        ).astype(jnp.bfloat16),
        "tp",
        scatter_dimension=0,
        tiled=True,
    ).astype(jnp.float32)
    key_sum = lax.psum(key_terms, "tp").reshape(2, KVH, HD, capacity)
    group_keys = lax.dynamic_index_in_dim(key_sum, key_group, 1, keepdims=False)
    query_heads = (
        (query_sum * inverse_rms[None, :]).astype(jnp.bfloat16).reshape(heads_local, HD, capacity)
    )
    key_values = (group_keys * inverse_rms[None, None, :]).astype(jnp.bfloat16)
    shard_ids = jnp.arange(ctx_count, dtype=jnp.int32)[:, None]
    key_positions = jnp.where(
        kept_rows < token_count, shard_ids * token_count + kept_rows, ctx_count * token_count
    ).reshape(-1)
    query_positions = jnp.where(is_valid, shard_index * token_count + own_rows, -1)
    score_scale = HD ** (-0.5)

    def advance(state, kv_block, block_positions):
        running_peak, running_total, running_acc = state
        scores = (
            jnp.einsum("hdq,dk->hqk", query_heads, kv_block[0], preferred_element_type=jnp.float32)
            * score_scale
        )
        allowed = block_positions[None, None, :] <= query_positions[None, :, None]
        scores = jnp.where(allowed, scores, MASKED_SCORE)
        new_peak = jnp.maximum(running_peak, jnp.max(scores, axis=2))
        exp_weights = jnp.where(allowed, jnp.exp(scores - new_peak[..., None]), 0.0)
        rescale = jnp.exp(running_peak - new_peak)
        new_total = running_total * rescale + jnp.sum(exp_weights, axis=2)
        mixed = jnp.einsum(
            "hqk,dk->hqd",
            exp_weights.astype(jnp.bfloat16),
            kv_block[1],
            preferred_element_type=jnp.float32,
        )
        return (new_peak, new_total, running_acc * rescale[..., None] + mixed)

    initial = (
        jnp.full((heads_local, capacity), MASKED_SCORE, jnp.float32),
        jnp.zeros((heads_local, capacity), jnp.float32),
        jnp.zeros((heads_local, capacity, HD), jnp.float32),
    )
    kv_piece = lax.all_gather(key_values, "ctx", axis=2, tiled=True)
    kv_count = kv_piece.shape[2]
    block_count = kv_count // capacity
    kv_blocks = jnp.transpose(kv_piece.reshape(2, HD, block_count, capacity), (2, 0, 1, 3))
    position_blocks = key_positions.reshape(block_count, capacity)

    def one_block(inner_state, element):
        kv_block, block_positions = element
        inner_state = advance(inner_state, kv_block, block_positions)
        return (inner_state, None)

    final_state, _ = lax.scan(one_block, initial, (kv_blocks, position_blocks))
    final_peak, final_total, final_acc = final_state
    safe_total = jnp.where(is_valid[None, :], final_total, 1.0)
    head_output = (final_acc / safe_total[..., None]).astype(jnp.bfloat16)
    heads_piece = lax.all_gather(head_output, "tp", axis=0, tiled=True)
    head_count = heads_piece.shape[0]
    out_rows = out_weight.reshape(head_count, HD, width_local)
    projected = jnp.einsum("hqd,hde->qe", heads_piece, out_rows, preferred_element_type=jnp.float32)
    row_update = (jax.nn.sigmoid(router_logit)[:, None] * projected).astype(jnp.bfloat16)
    target_rows = jnp.where(is_valid, own_rows, token_count)
    return jnp.zeros_like(hidden).at[target_rows].set(row_update, mode="drop")


def solution(mesh):
    return jax.shard_map(
        shards,
        mesh=mesh,
        in_specs=(
            P("ctx", "tp"),
            P("tp"),
            P("tp"),
            P("tp", None),
            P(None, "tp", None),
            P(None, "tp"),
            P(),
        ),
        out_specs=P("ctx", "tp"),
        check_vma=False,
    )
```

profile of v0, /device:TPU:0, one launch (start us, length us, event | category | flops | bytes accessed | tf_op | source)
XLA Modules:
  0.0 402.9 jit_solution(9573237296460204810)
XLA Ops:
  6.5 0.7 compare_select_fusion
  7.3 0.7 convert_element_type.34
  8.0 7.1 %gather_fusion = bf16[512,2048]{1,0:T(8,128)(2,1)S(1)} fusion(bf16[1024,2048]{1,0:T(8,128)(2,1)} %param.9, s32[1024]{0:T(1024)S(1)} %pad_clamp_fusion), kind=kCustom, calls=%fused_computation | custom fusion | bytes 4196352 | tf_op jit(solution)/shard_map/gather | solution.py:27
  15.1 5.9 %fusion.18 = f32[512,2,512]{0,2,1:T(8,128)} fusion(bf16[2,2048,512]{2,1,0:T(8,128)(2,1)} %param.13, bf16[512,2048]{1,0:T(8,128)(2,1)S(1)} %gather_fusion, f32[2048]{0:T(1024)S(1)} %convert_element_type.34), kind=kOutput, calls=%fused_computation.32 | convolution fusion | flops 2150629376 | bytes 8396800 | tf_op jit(solution)/shard_map/dot_general | solution.py:34
  21.0 13.7 %fusion.14 = bf16[4096,512]{0,1:T(8,128)(2,1)} fusion(bf16[2048,4096]{1,0:T(8,128)(2,1)} %param.12, bf16[512,2048]{1,0:T(8,128)(2,1)S(1)} %gather_fusion, f32[2048]{0:T(1024)S(1)} %convert_element_type.34), kind=kOutput, calls=%fused_computation.25 | convolution fusion | flops 8595177472 | bytes 23076864 | tf_op jit(solution)/shard_map/dot_general | solution.py:39
  34.9 0.6 copy-done.3
  35.5 0.5 fusion.16
  35.9 0.6 fusion.25
  36.6 14.0 %all-reduce = (f32[512]{0:T(512)S(1)}, f32[512]{0:T(512)S(1)}) all-reduce(f32[512]{0:T(512)S(1)} %fusion.16, f32[512]{0:T(512)S(1)} %bitcast.87), channel_id=1, replica_groups=mesh['ctx'=8,'tp'=4] {'tp'}, use_global_device_ids=true, to_apply=%region_3.4 | all-reduce | flops 1024 | bytes 8192 | tf_op jit(solution)/shard_map/psum | solution.py:32
  50.6 59.9 %all-reduce.3.cloned.1.call-done = f32[2,4,128,512]{3,2,1,0:T(8,128)} async-done(((f32[2,4,128,512]{3,2,1,0:T(8,128)}), f32[2,4,128,512]{3,2,1,0:T(8,128)}) %all-reduce.3.cloned.1.call-update) | async-done | bytes 2097168 | tf_op jit(solution)/shard_map/psum | solution.py:46
  110.6 1.1 constant_dynamic-slice_fusion.1
  111.9 0.8 fusion.24
  112.7 0.2 all-gather.5.cloned.1.call-start
  113.1 75.6 %reduce-scatter.2.cloned.1.call-done = bf16[1024,512]{0,1:T(8,128)(2,1)} async-done(((bf16[4096,512]{0,1:T(8,128)(2,1)}), bf16[1024,512]{0,1:T(8,128)(2,1)}) %reduce-scatter.2.cloned.1.call-update) | async-done | bytes 1048592 | tf_op jit(solution)/shard_map/reduce_scatter | solution.py:38
  188.7 1.5 multiply_convert_fusion
  190.2 0.5 copy.27
  190.8 28.3 %all-gather.3.cloned.1.call-done = bf16[2,128,4096]{1,2,0:T(8,128)(2,1)} async-done(((bf16[2,128,512]{1,2,0:T(8,128)(2,1)}), bf16[2,128,4096]{1,2,0:T(8,128)(2,1)}) %all-gather.3.cloned.1.call-update) | async-done | bytes 2097168 | tf_op jit(solution)/shard_map/all_gather | solution.py:84
  219.1 74.4 %while.15 = (s32[]{:T(128)}, f32[8,512]{1,0:T(8,128)S(1)}, f32[8,512]{1,0:T(8,128)S(1)}, f32[8,512,128]{2,1,0:T(8,128)}, s32[8,512]{1,0:T(8,128)S(1)}, /*index=5...) while((s32[]{:T(128)}, f32[8,512]{1,0:T(8,128)S(1)}, ...), condition=%wide.region_8.9_spmd.clone, body=%wide.region_5.8_spmd.clone.sunk | while | flops 1102860288 | bytes 49291448 | solution.py:95
  219.1 0.2 broadcast_compare_fusion.2
  219.3 1.0 dynamic-slice_bitcast_fusion.2
  220.3 1.5 fusion.41
  221.9 2.0 fusion.42
  223.9 3.1 fusion.44
  227.1 1.3 copy-done.1
  228.6 1.0 dynamic-slice_bitcast_fusion.2
  229.6 1.5 fusion.41
  231.2 2.0 fusion.42
  233.2 3.1 fusion.44
  236.4 1.3 copy-done.1
  237.9 1.0 dynamic-slice_bitcast_fusion.2
  238.9 1.5 fusion.41
  240.5 2.0 fusion.42
  242.6 3.1 fusion.44
  245.7 1.3 copy-done.1
  247.2 1.0 dynamic-slice_bitcast_fusion.2
  248.2 1.5 fusion.41
  249.8 2.0 fusion.42
  251.9 3.1 fusion.44
  255.0 1.3 copy-done.1
  256.5 1.0 dynamic-slice_bitcast_fusion.2
  257.5 1.5 fusion.41
  259.1 2.0 fusion.42
  261.2 3.1 fusion.44
  264.3 1.3 copy-done.1
  265.6 0.2 broadcast_compare_fusion.2
  265.8 1.0 dynamic-slice_bitcast_fusion.2
  266.8 1.5 fusion.41
  268.4 2.0 fusion.42
  270.5 3.1 fusion.44
  273.6 1.3 copy-done.1
  275.1 1.0 dynamic-slice_bitcast_fusion.2
  276.1 1.5 fusion.41
  277.7 2.0 fusion.42
  279.8 3.1 fusion.44
  282.9 1.3 copy-done.1
  284.4 1.0 dynamic-slice_bitcast_fusion.2
  285.4 1.5 fusion.41
  287.0 2.0 fusion.42
  289.1 3.1 fusion.44
  292.2 1.3 copy-done.1
  293.5 2.7 divide_convert_fusion
  296.3 80.9 %all-gather.5.cloned.1.call-done = bf16[32,512,128]{2,1,0:T(8,128)(2,1)} async-done(((bf16[8,512,128]{2,1,0:T(8,128)(2,1)}), bf16[32,512,128]{2,1,0:T(8,128)(2,1)}) %all-gather.5.cloned.1.call-update) | async-done | bytes 4194320 | tf_op jit(solution)/shard_map/all_gather | solution.py:99
  377.2 12.8 %fusion.17 = bf16[512,2048]{1,0:T(8,128)(2,1)S(1)} fusion(bf16[32,512,128]{2,1,0:T(8,128)(2,1)} %all-gather.5.cloned.1.call-done, bf16[32,128,2048]{2,1,0:T(8,128)(2,1)} %bitcast.90, f32[512]{0:T(512)S(1)} %add_divide_fusion), kind=kOutput, calls=%fused_computation.31 | convolution fusion | flops 8592031744 | bytes 23070720 | tf_op jit(solution)/shard_map/hqd,hde->qe/dot_general | solution.py:102
  390.1 6.3 %scatter_custom_fusion = bf16[1024,2048]{1,0:T(8,128)(2,1)} fusion(s32[512]{0:T(512)S(1)} %bitcast.89, bf16[512,2048]{1,0:T(8,128)(2,1)S(1)} %fusion.17, bf16[]{:T(256)} %constant.22.clone.1), kind=kCustom, calls=%fused_computation.36 | custom fusion | bytes 4194306 | tf_op jit(solution)/shard_map/scatter | solution.py:105
  (85 shorter events, 2.1 us)
Async XLA Ops:
  6.5 104.0 %all-reduce.3.cloned.1.call-start = ((), (), s32[]{:S(2)}) async-start(), calls=%async_computation.1 | async-start | bytes 4194304 | tf_op jit(solution)/shard_map/psum | solution.py:46
  21.0 167.7 %reduce-scatter.2.cloned.1.call-start = ((), (), s32[]{:S(2)}) async-start(), calls=%async_computation.3 | async-start | bytes 5242880 | tf_op jit(solution)/shard_map/reduce_scatter | solution.py:38
  34.8 0.7 copy-start.3
  34.8 78.2 %copy-start.2 = (s32[8,512]{1,0:T(8,128)S(1)}, s32[8,512]{1,0:T(8,128)}, u32[]{:S(2)}) copy-start(s32[8,512]{1,0:T(8,128)} %param.15) | copy-start | bytes 49156
  34.8 184.3 %all-gather.3.cloned.1.call-start = ((), (), s32[]{:S(2)}) async-start(), calls=%async_computation.2 | async-start | bytes 2359296 | tf_op jit(solution)/shard_map/all_gather | solution.py:84
  112.7 264.5 %all-gather.5.cloned.1.call-start = ((), (), s32[]{:S(2)}) async-start(), calls=%async_computation.4 | async-start | bytes 5242880 | tf_op jit(solution)/shard_map/all_gather | solution.py:99
  221.9 2.1 copy-start
  227.1 1.3 copy-start.1
  231.2 2.1 copy-start
  236.4 1.3 copy-start.1
  240.5 2.1 copy-start
  245.7 1.3 copy-start.1
  249.8 2.1 copy-start
  255.0 1.3 copy-start.1
  259.1 2.1 copy-start
  264.3 1.3 copy-start.1
  268.4 2.1 copy-start
  273.6 1.3 copy-start.1
  277.7 2.1 copy-start
  282.9 1.3 copy-start.1
  287.0 2.1 copy-start
  292.2 1.3 copy-start.1
Sparse Core Ops, SparseCore 0:
  21.1 89.4 all-reduce.2
  113.0 75.7 reduce-scatter.1
  190.6 28.3 all-gather.2
  296.4 80.7 all-gather.4
where the time goes:
time: 404 us; the launch traced here: 403 us
  waiting for transfers between devices  245 us (61%)
  matrix products  70.5 us (17%)
  local copies, waits for them, and re-layouts  33.9 us (8%)
  other arithmetic  25.3 us (6%)
  blocking collectives  14 us (3%)
  between operations  13.3 us (3%)
    all_gather x1, waiting for transfers between devices, shards(): heads_piece = lax.all_gather(head_output, 'tp', axis=0, tiled=True)  80.9 us
    reduce_scatter x1, waiting for transfers between devices, shards(): lax.psum_scatter(lax.dot_general(query_weight, normed, (((0,), (1,)), (()...  75.6 us
    psum x1, waiting for transfers between devices, shards(): key_sum = lax.psum(key_terms, 'tp').reshape(2, KVH, HD, capacity)  59.9 us
    all_gather x1, waiting for transfers between devices, shards(): kv_piece = lax.all_gather(key_values, 'ctx', axis=2, tiled=True)  28.3 us
    dot_general x8, matrix products, advance(): jnp.einsum('hqk,dk->hqd', exp_weights.astype(jnp.bfloat16), kv_block[1],...  25.1 us
    reduce_sum x8, other arithmetic, advance(): new_total = running_total * rescale + jnp.sum(exp_weights, axis=2)  16.3 us
    psum x1, blocking collectives, shards(): square_sum, router_logit = lax.psum((square_part, router_part), 'tp')  14 us
    dot_general x1, matrix products, shards(): lax.dot_general(query_weight, normed, (((0,), (1,)), ((), ())), preferred...  13.7 us
  transfers between devices with their start and end apart: 4, of which 4 were waited for; matrix products, arithmetic and copies ran while one was open for 5% of the time, Pallas kernels for 0%

commit v1 on v0

v1 whole, which is shorter than its diff:
```python
import functools

import jax
import jax.numpy as jnp
from jax import lax
from jax.experimental import pallas as pl
from jax.experimental.pallas import tpu as pltpu
from jax.sharding import PartitionSpec as P

D = 8192
H = 32
KVH = 4
HD = 128
EPSILON = 1e-05
MASKED_SCORE = -1e30
BF16 = jnp.bfloat16
F32 = jnp.float32


def attention_kernel(ctx_count, keep, q_ref, k_ref, v_ref, me_ref, o_ref):
    heads = q_ref.shape[1] // HD
    me = me_ref[0]
    rows = keep // 2
    for half in range(2):
        span = rows * (half + 1)
        q_rank = (lax.broadcasted_iota(jnp.int32, (rows, span), 0) + half * rows) * ctx_count + me
        slot = lax.broadcasted_iota(jnp.int32, (rows, span), 1) * ctx_count
        masks = [slot + c <= q_rank for c in range(ctx_count)]
        for h in range(heads):
            q = q_ref[pl.ds(half * rows, rows), pl.ds(h * HD, HD)]
            scores = []
            for c in range(ctx_count):
                s = lax.dot_general(
                    q, k_ref[c, pl.ds(0, span), :], (((1,), (1,)), ((), ())),
                    preferred_element_type=F32,
                ) * (HD ** -0.5)
                scores.append(jnp.where(masks[c], s, MASKED_SCORE))
            peak = functools.reduce(jnp.maximum, scores)
            peak = jnp.max(peak, axis=1, keepdims=True)
            total = jnp.zeros((rows, span), F32)
            mixed = jnp.zeros((rows, HD), F32)
            for c in range(ctx_count):
                w = jnp.exp(scores[c] - peak)
                total = total + w
                mixed = mixed + jnp.dot(
                    w.astype(BF16), v_ref[c, pl.ds(0, span), :], preferred_element_type=F32
                )
            total = jnp.sum(total, axis=1, keepdims=True)
            o_ref[pl.ds(half * rows, rows), pl.ds(h * HD, HD)] = (mixed / total).astype(BF16)


def attention(q, k, v, me, ctx_count, keep):
    return pl.pallas_call(
        functools.partial(attention_kernel, ctx_count, keep),
        out_shape=jax.ShapeDtypeStruct(q.shape, BF16),
        in_specs=[pl.BlockSpec(memory_space=pltpu.VMEM)] * 3
        + [pl.BlockSpec(memory_space=pltpu.SMEM)],
        out_specs=pl.BlockSpec(memory_space=pltpu.VMEM),
        compiler_params=pltpu.CompilerParams(vmem_limit_bytes=48 * 2**20),
        name="attention",
    )(q, k, v, me)


def one_hot(index, count, axis):
    shape = (count,) + index.shape if axis == 0 else index.shape + (count,)
    iota = lax.broadcasted_iota(jnp.int32, shape, 0 if axis == 0 else len(shape) - 1)
    target = index[None] if axis == 0 else index[..., None]
    return (iota == target).astype(BF16)


def shards(hidden, norm_gain, router_weight, query_weight, key_value_weight, out_weight, kept_rows):
    me = lax.axis_index("ctx")
    ctx_count = lax.axis_size("ctx")
    tp_count = lax.axis_size("tp")
    tp_index = lax.axis_index("tp")
    token_count, width = hidden.shape
    capacity = kept_rows.shape[1]
    keep = capacity // 2
    part = capacity // ctx_count
    heads = H // tp_count

    counts = jnp.sum((kept_rows < token_count).astype(jnp.int32), axis=1)
    starts = jnp.cumsum(counts) - counts
    ids = jnp.arange(ctx_count, dtype=jnp.int32)
    slots = jnp.arange(part, dtype=jnp.int32)

    first = (ids - starts[me]) % ctx_count
    send_index = first[:, None] + ctx_count * slots[None, :]
    own_rows = lax.dynamic_index_in_dim(kept_rows, me, 0, keepdims=False)
    send_rows = jnp.take(own_rows, send_index.reshape(-1), axis=0)
    pick = one_hot(send_rows, token_count, 1)
    sent = jnp.dot(pick, hidden, preferred_element_type=F32).astype(BF16)
    got = lax.all_to_all(sent.reshape(ctx_count, part, width), "ctx", 0, 0).reshape(capacity, width)

    come_first = (me - starts) % ctx_count
    come_slot = (starts + come_first)[:, None] // ctx_count + slots[None, :]
    come_valid = come_first[:, None] + ctx_count * slots[None, :] < counts[:, None]
    place = jnp.where(come_valid, come_slot, keep).reshape(-1)
    compact = one_hot(place, keep, 0)
    kept = jnp.dot(compact, got, preferred_element_type=F32).astype(BF16)

    widened = kept.astype(F32)
    square_part = jnp.sum(widened * widened, axis=1)
    router_part = jnp.dot(kept, router_weight, preferred_element_type=F32)
    normed = (widened * norm_gain.astype(F32)).astype(BF16)
    square_sum, router_logit = lax.psum((square_part, router_part), "tp")
    inverse_rms = lax.rsqrt(square_sum / D + EPSILON)

    q_terms = lax.dot_general(
        query_weight, normed, (((0,), (1,)), ((), ())), preferred_element_type=F32
    ).astype(BF16).reshape(tp_count, heads * HD, keep)
    kv_terms = lax.dot_general(
        key_value_weight, normed, (((1,), (1,)), ((), ())), preferred_element_type=F32
    ).astype(BF16).reshape(2, KVH, HD, keep)
    group_of = [t * heads // (H // KVH) for t in range(tp_count)]
    kv_terms = jnp.stack([kv_terms[:, g] for g in group_of]).reshape(tp_count, 2 * HD, keep)
    terms = jnp.concatenate([q_terms, kv_terms], axis=1)
    sums = lax.psum_scatter(terms, "tp", scatter_dimension=0, tiled=False)
    scaled = (sums.astype(F32) * inverse_rms[None, :]).astype(BF16).T
    queries = scaled[:, : heads * HD]
    key_values = lax.all_gather(scaled[:, heads * HD :], "ctx", axis=0, tiled=False)
    head_output = attention(
        queries, key_values[:, :, :HD], key_values[:, :, HD:], me.reshape(1), ctx_count, keep
    )

    gathered = lax.all_gather(head_output, "tp", axis=0, tiled=False)
    projected = jnp.einsum(
        "tqe,tef->qf", gathered, out_weight.reshape(tp_count, heads * HD, width),
        preferred_element_type=F32,
    )
    row_update = (jax.nn.sigmoid(router_logit)[:, None] * projected).astype(BF16)

    back = lax.dot_general(
        compact, row_update, (((0,), (0,)), ((), ())), preferred_element_type=F32
    ).astype(BF16)
    home = lax.all_to_all(back.reshape(ctx_count, part, width), "ctx", 0, 0).reshape(capacity, width)
    return lax.dot_general(
        pick, home, (((0,), (0,)), ((), ())), preferred_element_type=F32
    ).astype(BF16)


def solution(mesh):
    return jax.shard_map(
        shards,
        mesh=mesh,
        in_specs=(
            P("ctx", "tp"),
            P("tp"),
            P("tp"),
            P("tp", None),
            P(None, "tp", None),
            P(None, "tp"),
            P(),
        ),
        out_specs=P("ctx", "tp"),
        check_vma=False,
    )
```

time: 404 us -> 261 us (0.65)
  waiting for transfers between devices: 245 us -> 134 us
  matrix products: 70.5 us -> 35.4 us
  blocking collectives: 14 us -> 42.3 us
  other arithmetic: 25.3 us -> 5.5 us
  local copies, waits for them, and re-layouts: 33.9 us -> 15.8 us
  Pallas kernels: 0 us -> 8.82 us
  starting transfers between devices: 0.31 us -> 5.6 us
    psum x1 -> x0, waiting for transfers between devices: 59.9 us -> none  [shards(): key_sum = lax.psum(key_terms, 'tp').reshape(2, KVH, HD, capacity)]
    all_gather x2, waiting for transfers between devices: 109 us -> 69.1 us  [the longest x1 46.1 us: shards(): gathered = lax.all_gather(head_output, 'tp', axis=0, tiled=False)]
    reduce_scatter x1, waiting for transfers between devices: 75.6 us -> 38.4 us  [shards(): sums = lax.psum_scatter(terms, 'tp', scatter_dimension=0, tiled=False)]
    all_to_all x0 -> x1, blocking collectives: none -> 30 us  [shards(): lax.all_to_all(back.reshape(ctx_count, part, width), 'ctx', 0, 0)]
    dot_general x18 -> x5, matrix products: 51 us -> 23.6 us  [the longest x1 11.4 us: shards(): lax.dot_general(compact, row_update, (((0,), (0,)), ((), ())), preferred_...]
    all_to_all x0 -> x1, waiting for transfers between devices: none -> 26.5 us  [shards(): lax.all_to_all(sent.reshape(ctx_count, part, width), 'ctx', 0, 0)]
    reduce_sum x9 -> x1, other arithmetic: 16.8 us -> 0.83 us  [shards(): counts = jnp.sum((kept_rows < token_count).astype(jnp.int32), axis=1)]
    while x40 -> x0, local copies, waits for them, and re-layouts: 10.3 us -> none
  transfers between devices with their start and end apart: 4 -> 4, of which waited for: 4 -> 4; matrix products, arithmetic and copies ran while one was open for 5% -> 0% of each run, Pallas kernels for 0% -> 0%
where the time goes in v1:
time: 261 us
  waiting for transfers between devices  134 us (51%)
  blocking collectives  42.3 us (16%)
  matrix products  35.4 us (14%)
  local copies, waits for them, and re-layouts  15.8 us (6%)
  between operations  13.3 us (5%)
  Pallas kernels  8.82 us (3%)
  starting transfers between devices  5.6 us (2%)
  other arithmetic  5.5 us (2%)
    all_gather x1, waiting for transfers between devices, shards(): gathered = lax.all_gather(head_output, 'tp', axis=0, tiled=False)  46.1 us
    reduce_scatter x1, waiting for transfers between devices, shards(): sums = lax.psum_scatter(terms, 'tp', scatter_dimension=0, tiled=False)  38.4 us
    all_to_all x1, blocking collectives, shards(): lax.all_to_all(back.reshape(ctx_count, part, width), 'ctx', 0, 0)  30 us
    all_to_all x1, waiting for transfers between devices, shards(): lax.all_to_all(sent.reshape(ctx_count, part, width), 'ctx', 0, 0)  26.5 us
    all_gather x1, waiting for transfers between devices, shards(): lax.all_gather(scaled[:, heads * HD:], 'ctx', axis=0, tiled=False)  23 us
    psum x1, blocking collectives, shards(): square_sum, router_logit = lax.psum((square_part, router_part), 'tp')  12.3 us
    dot_general x1, matrix products, shards(): lax.dot_general(compact, row_update, (((0,), (0,)), ((), ())), preferred_...  11.4 us
    pallas_call x1, Pallas kernels, attention(): pl.pallas_call(functools.partial(attention_kernel, ctx_count, keep), out_...  8.82 us
  transfers between devices with their start and end apart: 4, of which 4 were waited for; matrix products, arithmetic and copies ran while one was open for 0% of the time, Pallas kernels for 0%

profile of v1, /device:TPU:0, one launch (start us, length us, event | category | flops | bytes accessed | tf_op | source)
XLA Modules:
  0.0 260.7 jit_solution(10365099649833777355)
XLA Ops:
  6.5 0.8 convert_reduce_fusion
  7.4 0.2 reduce-window.7
  7.6 0.7 constant_dynamic-slice_fusion
  8.3 0.6 dynamic_slice.7
  8.9 0.7 and_select_fusion.3
  9.6 0.1 add_select_fusion
  9.6 0.1 add.154
  9.7 0.1 add.151
  9.8 3.5 %gather_fusion = s32[512]{0:T(512)S(1)} fusion(s32[512]{0:T(512)S(1)} %bitcast.56, s32[1024]{0:T(1024)S(1)} %pad_clamp_fusion), kind=kCustom, calls=%fused_computation | custom fusion | bytes 6144 | tf_op jit(solution)/shard_map/jit(_take)/gather | solution.py:90
  13.3 5.9 %convolution_convert_fusion.3 = bf16[512,2048]{1,0:T(8,128)(2,1)} fusion(bf16[1024,2048]{1,0:T(8,128)(2,1)} %param.7, s32[512]{0:T(512)S(1)} %and_select_fusion.2), kind=kOutput, calls=%fused_computation.5 | convolution fusion | flops 2149056512 | bytes 6293504 | tf_op jit(solution)/shard_map/dot_general | solution.py:92
  19.2 0.0 copy-start
  19.2 5.3 %all-to-all-start = ((bf16[8,64,2048]{2,1,0:T(8,128)(2,1)}), bf16[8,64,2048]{2,1,0:T(8,128)(2,1)S(1)}, u32[]{:S(2)}, u32[]{:S(2)}) async-start(bf16[8,64,2048]{2,1,0:T(8,128)(2,1)} %bitcast.59), calls=%async_computation | async-start | bytes 4194304 | tf_op jit(solution)/shard_map/all_to_all | solution.py:93
  24.5 0.0 reduce-scatter.2.cloned.1.call-start
  24.5 0.1 select_n.83
  24.6 0.0 copy-done
  24.6 26.5 %all-to-all-done = bf16[8,64,2048]{2,1,0:T(8,128)(2,1)S(1)} async-done(((bf16[8,64,2048]{2,1,0:T(8,128)(2,1)}), bf16[8,64,2048]{2,1,0:T(8,128)(2,1)S(1)}, u32[]{:S(2)}, u32[]{:S(2)}) %all-to-all-start) | async-done | bytes 2097184 | tf_op jit(solution)/shard_map/all_to_all | solution.py:93
  51.1 1.4 fusion.4
  52.5 3.4 %fusion.6 = bf16[2,512,256]{1,2,0:T(8,128)(2,1)S(1)} fusion(bf16[2,2048,512]{2,1,0:T(8,128)(2,1)} %param.11, bf16[256,2048]{1,0:T(8,128)(2,1)S(1)} %get-tuple-element.19, f32[2048]{0:T(1024)S(1)} %convert_element_type.54), kind=kOutput, calls=%fused_computation.19 | convolution fusion | flops 1075576832 | bytes 5775360 | tf_op jit(solution)/shard_map/dot_general | solution.py:112
  56.0 0.1 reshape.224
  56.1 0.8 fusion.18
  56.9 0.2 copy.18
  57.1 0.1 stack.11
  57.2 0.2 copy.20
  57.4 0.1 stack.13
  57.5 0.2 copy.19
  57.7 0.1 stack.12
  57.8 0.2 copy.21
  58.0 0.7 stack.14
  58.7 8.4 %fusion = bf16[4096,256]{0,1:T(8,128)(2,1)S(1)} fusion(bf16[2048,4096]{1,0:T(8,128)(2,1)} %param.10, bf16[256,2048]{1,0:T(8,128)(2,1)S(1)} %get-tuple-element.19, f32[2048]{0:T(1024)S(1)} %convert_element_type.54), kind=kOutput, calls=%fused_computation.2 | convolution fusion | flops 4297588736 | bytes 19931136 | tf_op jit(solution)/shard_map/dot_general | solution.py:109
  67.2 2.5 copy.12
  69.6 3.0 %copy.17 = bf16[4,1024,256]{1,2,0:T(8,128)(2,1)S(1)} copy(bf16[4,1024,256]{2,1,0:T(8,128)(2,1)} %bitcast.57) | data formatting | bytes 4194304 | tf_op jit(solution)/shard_map/reshape | solution.py:111
  72.6 2.4 maximum_maximum_fusion
  75.0 0.0 copy-start.1
  75.0 0.0 copy-start.2
  75.0 0.0 reduce-scatter.2.cloned.1.call-update
  75.1 0.0 all-gather.5.cloned.1.call-start
  75.1 0.6 copy-done.1
  75.7 0.4 fusion.19
  76.1 0.0 copy-done.2
  76.1 12.3 %all-reduce = (f32[256]{0:T(256)S(1)}, f32[256]{0:T(256)S(1)}) all-reduce(f32[256]{0:T(256)S(1)} %copy-done.2, f32[256]{0:T(256)S(1)} %bitcast.65), channel_id=1, replica_groups=mesh['ctx'=8,'tp'=4] {'tp'}, use_global_device_ids=true, to_apply=%region_5.6 | all-reduce | flops 512 | bytes 4096 | tf_op jit(solution)/shard_map/psum | solution.py:106
  88.4 38.4 %reduce-scatter.2.cloned.1.call-done = bf16[1,1280,256]{1,2,0:T(8,128)(2,1)} async-done(((bf16[4,1280,256]{1,2,0:T(8,128)(2,1)}), bf16[1,1280,256]{1,2,0:T(8,128)(2,1)}) %reduce-scatter.2.cloned.1.call-update) | async-done | bytes 655376 | tf_op jit(solution)/shard_map/reduce_scatter | solution.py:118
  126.8 1.3 fusion.12
  128.0 0.7 slice.39
  128.7 0.0 all-gather.5.cloned.1.call-update
  128.7 0.2 all-gather.7.cloned.1.call-start
  128.9 0.1 slice.38.q_ref
  129.0 23.0 %all-gather.5.cloned.1.call-done = bf16[2048,256]{1,0:T(8,128)(2,1)} async-done(((bf16[256,256]{1,0:T(8,128)(2,1)}), bf16[2048,256]{1,0:T(8,128)(2,1)}) %all-gather.5.cloned.1.call-update) | async-done | bytes 1048592 | tf_op jit(solution)/shard_map/all_gather | solution.py:121
  152.0 1.3 fusion.17
  153.3 8.8 %attention.1 = bf16[256,1024]{1,0:T(8,128)(2,1)} custom-call(bf16[256,1024]{1,0:T(8,128)(2,1)S(1)} %slice.38.q_ref, bf16[8,256,128]{2,1,0:T(8,128)(2,1)S(1)} %get-tuple-element.11.k_ref, bf16[8,256,128]{2,1,0:T(8,128)(2,1)S(1)} %get-tuple-element.10.v_ref, s32[1]{0:T(128)} %bitcast.15.me_ref), custom_call_target="tpu_custom_call" | custom-call | tf_op jit(solution)/shard_map/attention/pallas_call | solution.py:53
  162.1 0.0 all-gather.7.cloned.1.call-update
  162.2 46.1 %all-gather.7.cloned.1.call-done = bf16[1024,1024]{1,0:T(8,128)(2,1)} async-done(((bf16[256,1024]{1,0:T(8,128)(2,1)}), bf16[1024,1024]{1,0:T(8,128)(2,1)}) %all-gather.7.cloned.1.call-update) | async-done | bytes 2097168 | tf_op jit(solution)/shard_map/all_gather | solution.py:126
  208.3 11.4 %convolution_convert_fusion.2 = bf16[512,2048]{1,0:T(8,128)(2,1)S(1)} fusion(bf16[4,256,1024]{2,1,0:T(8,128)(2,1)} %bitcast.67, bf16[4,1024,2048]{2,1,0:T(8,128)(2,1)} %bitcast.66, f32[256]{0:T(256)S(1)} %add_divide_fusion, s32[512]{0:T(512)S(1)} %select_n.83), kind=kOutput, calls=%fused_computation.4 | convolution fusion | flops 4834066432 | bytes 20974592 | tf_op jit(solution)/shard_map/dot_general | solution.py:133
  219.7 30.0 %all_to_all.10 = bf16[8,64,2048]{2,1,0:T(8,128)(2,1)S(1)} all-to-all(bf16[8,64,2048]{2,1,0:T(8,128)(2,1)S(1)} %bitcast.60), channel_id=1, replica_groups=mesh['ctx'=8,'tp'=4] {'ctx'}, dimensions={0} | all-to-all | bytes 4194304 | tf_op jit(solution)/shard_map/all_to_all | solution.py:136
  249.7 4.5 %convolution_convert_fusion.1 = bf16[1024,2048]{1,0:T(8,128)(2,1)} fusion(bf16[512,2048]{1,0:T(8,128)(2,1)S(1)} %bitcast.61, s32[512]{0:T(512)S(1)} %and_select_fusion.2), kind=kOutput, calls=%fused_computation.3 | convolution fusion | flops 2150105088 | bytes 6293504 | tf_op jit(solution)/shard_map/dot_general | solution.py:137
  (9 shorter events, 0.1 us)
Async XLA Ops:
  19.2 5.4 %copy-start = (bf16[2048]{0:T(1024)(128)(2,1)S(1)}, bf16[2048]{0:T(1024)(128)(2,1)}, u32[]{:S(2)}) copy-start(bf16[2048]{0:T(1024)(128)(2,1)} %param.8) | copy-start | bytes 12292
  19.2 31.9 %all-to-all-start = ((bf16[8,64,2048]{2,1,0:T(8,128)(2,1)}), bf16[8,64,2048]{2,1,0:T(8,128)(2,1)S(1)}, u32[]{:S(2)}, u32[]{:S(2)}) async-start(bf16[8,64,2048]{2,1,0:T(8,128)(2,1)} %bitcast.59), calls=%async_computation | async-start | bytes 4194304 | tf_op jit(solution)/shard_map/all_to_all | solution.py:93
  24.5 102.3 %reduce-scatter.2.cloned.1.call-start = ((), (), s32[]{:S(2)}) async-start(), calls=%async_computation.3 | async-start | bytes 3276800 | tf_op jit(solution)/shard_map/reduce_scatter | solution.py:118
  75.0 0.7 copy-start.1
  75.0 1.1 copy-start.2
  75.1 77.0 %all-gather.5.cloned.1.call-start = ((), (), s32[]{:S(2)}) async-start(), calls=%async_computation.4 | async-start | bytes 1179648 | tf_op jit(solution)/shard_map/all_gather | solution.py:121
  128.7 79.5 %all-gather.7.cloned.1.call-start = ((), (), s32[]{:S(2)}) async-start(), calls=%async_computation.5 | async-start | bytes 2621440 | tf_op jit(solution)/shard_map/all_gather | solution.py:126
Sparse Core Ops, SparseCore 0:
  75.2 51.5 reduce-scatter.1
  128.8 23.1 all-gather.4
  162.3 45.9 all-gather.6

commit v2 on v1

v2 whole, which is shorter than its diff:
```python
import functools

import jax
import jax.numpy as jnp
from jax import lax
from jax.experimental import pallas as pl
from jax.experimental.pallas import tpu as pltpu
from jax.sharding import PartitionSpec as P

D = 8192
H = 32
KVH = 4
HD = 128
EPSILON = 1e-05
MASKED_SCORE = -1e30
BF16 = jnp.bfloat16
F32 = jnp.float32


MESH = pl.DeviceIdType.MESH
ROWS = 256
WIDE = 2 * HD
KV_CHUNKS = 2
Q_CHUNKS = H // 4
CHUNKS = KV_CHUNKS + Q_CHUNKS


def greet(ctx_partners, tp_partners):
    barrier = pltpu.get_barrier_semaphore()
    for c in ctx_partners:
        pl.semaphore_signal(barrier, inc=1, device_id={"ctx": c}, device_id_type=MESH)
    for t in tp_partners:
        pl.semaphore_signal(barrier, inc=1, device_id={"tp": t}, device_id_type=MESH)
    pl.semaphore_wait(barrier, len(ctx_partners) + len(tp_partners))


def project_kernel(
    ctx_count, tp_count, x_ref, stats_ref, wq_ref, wkv_ref, q_ref, kv_ref, logit_ref,
    weights, sent, got, stats, scale, weight_sem, send_sem, recv_sem,
    stat_send, stat_recv, kv_send, kv_recv, pair_send, pair_recv,
):
    me, z = lax.axis_index("ctx"), lax.axis_index("tp")
    last = tp_count - 1
    twin = me + 1 - 2 * (me % 2)
    peers = [(me + 2 * k) % ctx_count for k in range(1, ctx_count // 2)]
    others = [(z + k) % tp_count for k in range(1, tp_count)]

    def weight_copy(half, i):
        columns = pl.ds(half * WIDE, WIDE)
        if i < KV_CHUNKS:
            source = wkv_ref.at[i, :, columns]
        else:
            source = wq_ref.at[:, pl.ds((half * Q_CHUNKS + i - KV_CHUNKS) * WIDE, WIDE)]
        return pltpu.make_async_copy(source, weights.at[half, i], weight_sem.at[half, i])

    for i in range(CHUNKS):
        for half in (1, 0):
            weight_copy(half, i).start()

    greet(peers + [twin], others)

    def stat_copy(k):
        return pltpu.make_async_remote_copy(
            src_ref=stats_ref, dst_ref=stats.at[z], send_sem=stat_send.at[k],
            recv_sem=stat_recv.at[k], device_id={"tp": others[k]}, device_id_type=MESH,
        )

    for k in range(tp_count - 1):
        stat_copy(k).start()

    def kv_copy(k, part):
        return pltpu.make_async_remote_copy(
            src_ref=kv_ref.at[me, part], dst_ref=kv_ref.at[me, part],
            send_sem=kv_send.at[k, part], recv_sem=kv_recv.at[k, part],
            device_id={"ctx": peers[k]}, device_id_type=MESH,
        )

    def pair_copy(k):
        origin = (me + ctx_count - 2 * k) % ctx_count
        return pltpu.make_async_remote_copy(
            src_ref=kv_ref.at[origin], dst_ref=kv_ref.at[origin],
            send_sem=pair_send.at[k], recv_sem=pair_recv.at[k],
            device_id={"ctx": twin}, device_id_type=MESH,
        )

    def chain(half, i):
        target = jnp.minimum(z + 1, last) if half == 1 else jnp.maximum(z - 1, 0)
        return pltpu.make_async_remote_copy(
            src_ref=sent.at[half, i], dst_ref=got.at[half, i],
            send_sem=send_sem.at[half, i], recv_sem=recv_sem.at[half, i],
            device_id={"tp": target}, device_id_type=MESH,
        )

    at_first = (z == last, z == 0)
    at_final = (z == 0, z == last)

    stats[z] = stats_ref[...]
    for k in range(tp_count - 1):
        stat_copy(k).wait()
    total = stats[0]
    for t in range(1, tp_count):
        total = total + stats[t]
    inverse = lax.rsqrt(total[0:1] / D + EPSILON)
    scale[...] = jnp.broadcast_to(inverse, (WIDE, ROWS)).T
    logit_ref[...] = jnp.broadcast_to(total[1:2], (HD, ROWS)).T

    def step(i, carry):
        for half in (1, 0):
            pltpu.make_async_copy(
                wkv_ref.at[0, :, pl.ds(0, WIDE)], weights.at[half, i], weight_sem.at[half, i]
            ).wait()
            term = jnp.dot(x_ref[...], weights[half, i], preferred_element_type=F32)
            sent[half, i] = term.astype(BF16)

            @pl.when(jnp.logical_not(at_first[half]))
            def _():
                chain(half, i).wait_recv()
                sent[half, i] = (term + got[half, i].astype(F32)).astype(BF16)

            @pl.when(jnp.logical_not(at_final[half]))
            def _():
                chain(half, i).start()

            @pl.when(at_final[half])
            def _():
                done = ((term + got[half, i].astype(F32)) * scale[...]).astype(BF16)

                @pl.when(i < KV_CHUNKS)
                def _():
                    part = jnp.minimum(i, KV_CHUNKS - 1)
                    kv_ref[me, part] = done
                    for k in range(len(peers)):
                        kv_copy(k, part).start()

                @pl.when(i >= KV_CHUNKS)
                def _():
                    q_ref[jnp.maximum(i - KV_CHUNKS, 0)] = done

        return carry

    lax.fori_loop(0, CHUNKS, step, 0)

    @pl.when(jnp.logical_or(z == 0, z == last))
    def _():
        pair_copy(0).start()
        for k in range(len(peers)):
            for part in range(KV_CHUNKS):
                kv_copy(k, part).wait()
            pair_copy(k + 1).start()
        for k in range(len(peers) + 1):
            pair_copy(k).wait()

    for half in (0, 1):
        @pl.when(jnp.logical_not(at_final[half]))
        def _():
            for i in range(CHUNKS):
                chain(half, i).wait_send()


def project(normed, stats, query_weight, key_value_weight, ctx_count, tp_count):
    width = normed.shape[1]
    vmem = pl.BlockSpec(memory_space=pltpu.VMEM)
    hbm = pl.BlockSpec(memory_space=pl.ANY)
    dma = pltpu.SemaphoreType.DMA
    return pl.pallas_call(
        functools.partial(project_kernel, ctx_count, tp_count),
        out_shape=(
            jax.ShapeDtypeStruct((Q_CHUNKS, ROWS, WIDE), BF16),
            jax.ShapeDtypeStruct((ctx_count, KV_CHUNKS, ROWS, WIDE), BF16),
            jax.ShapeDtypeStruct((ROWS, HD), F32),
        ),
        in_specs=[vmem, vmem, hbm, hbm],
        out_specs=(vmem, vmem, vmem),
        scratch_shapes=[
            pltpu.VMEM((2, CHUNKS, width, WIDE), BF16),
            pltpu.VMEM((2, CHUNKS, ROWS, WIDE), BF16),
            pltpu.VMEM((2, CHUNKS, ROWS, WIDE), BF16),
            pltpu.VMEM((tp_count, 8, ROWS), F32),
            pltpu.VMEM((ROWS, WIDE), F32),
            dma((2, CHUNKS)),
            dma((2, CHUNKS)),
            dma((2, CHUNKS)),
            dma((tp_count - 1,)),
            dma((tp_count - 1,)),
            dma((ctx_count // 2 - 1, KV_CHUNKS)),
            dma((ctx_count // 2 - 1, KV_CHUNKS)),
            dma((ctx_count // 2,)),
            dma((ctx_count // 2,)),
        ],
        compiler_params=pltpu.CompilerParams(
            collective_id=0, has_side_effects=True, vmem_limit_bytes=52 * 2**20
        ),
        name="project_and_sum",
    )(normed, stats, query_weight, key_value_weight)


def attend_kernel(
    ctx_count, tp_count, q_ref, kv_ref, logit_ref, wo_ref, o_ref,
    weights, heads, acc, weight_sem, send_sem, recv_sem,
):
    me, z = lax.axis_index("ctx"), lax.axis_index("tp")
    last = tp_count - 1

    def weight_copy(half, i):
        rows = pl.ds((half * Q_CHUNKS + i) * WIDE, WIDE)
        return pltpu.make_async_copy(wo_ref.at[rows, :], weights.at[half, i], weight_sem.at[half, i])

    for i in range(Q_CHUNKS):
        for half in (0, 1):
            weight_copy(half, i).start()

    greet([], [(z + k) % tp_count for k in range(1, tp_count)])

    def chain(half, i):
        target = jnp.minimum(z + 1, last) if half == 0 else jnp.maximum(z - 1, 0)
        return pltpu.make_async_remote_copy(
            src_ref=heads.at[half, i], dst_ref=heads.at[half, i],
            send_sem=send_sem.at[half, i], recv_sem=recv_sem.at[half, i],
            device_id={"tp": target}, device_id_type=MESH,
        )

    at_first = (z == 0, z == last)
    at_final = (z == last, z == 0)
    acc[...] = jnp.zeros_like(acc)

    def multiply(half, i):
        weight_copy(half, i).wait()
        acc[...] += jnp.dot(heads[half, i], weights[half, i], preferred_element_type=F32)

    def attend(half, i):
        column = pl.ds(pl.multiple_of(i // (Q_CHUNKS // 2) * HD, HD), HD)
        rows = ROWS // 2
        for block in range(2):
            span = rows * (block + 1)
            q_rank = (lax.broadcasted_iota(jnp.int32, (rows, span), 0) + block * rows) * ctx_count + me
            q_rank = jnp.concatenate([q_rank, q_rank], axis=0)
            slot = lax.broadcasted_iota(jnp.int32, (2 * rows, span), 1) * ctx_count
            q = q_ref[i, pl.ds(block * rows, rows), :]
            q = jnp.concatenate([q[:, :HD], q[:, HD:]], axis=0)
            scores = []
            for c in range(ctx_count):
                s = lax.dot_general(
                    q, kv_ref[c, 0, pl.ds(0, span), column], (((1,), (1,)), ((), ())),
                    preferred_element_type=F32,
                ) * (HD ** -0.5)
                scores.append(jnp.where(slot + c <= q_rank, s, MASKED_SCORE))
            peak = jnp.max(functools.reduce(jnp.maximum, scores), axis=1, keepdims=True)
            total = jnp.zeros((2 * rows, span), F32)
            mixed = jnp.zeros((2 * rows, HD), F32)
            for c in range(ctx_count):
                w = jnp.exp(scores[c] - peak)
                total = total + w
                mixed = mixed + jnp.dot(
                    w.astype(BF16), kv_ref[c, 1, pl.ds(0, span), column], preferred_element_type=F32
                )
            result = (mixed / jnp.sum(total, axis=1, keepdims=True)).astype(BF16)
            here = pl.ds(block * rows, rows)
            heads[half, i, here, :] = jnp.concatenate([result[:rows], result[rows:]], axis=1)

    for half in (0, 1):
        @pl.when(at_first[half])
        def _():
            def own(i, carry):
                attend(half, i)
                chain(half, i).start()
                multiply(half, i)
                return carry

            lax.fori_loop(0, Q_CHUNKS, own, 0)

    def rest(i, carry):
        for half in (0, 1):
            @pl.when(jnp.logical_not(at_first[half]))
            def _():
                chain(half, i).wait_recv()

                @pl.when(jnp.logical_not(at_final[half]))
                def _():
                    chain(half, i).start()

                multiply(half, i)

        return carry

    lax.fori_loop(0, Q_CHUNKS, rest, 0)
    gate = jax.nn.sigmoid(logit_ref[:, 0:1])
    o_ref[...] = (gate * acc[...]).astype(BF16)

    for half in (0, 1):
        @pl.when(jnp.logical_not(at_final[half]))
        def _():
            for i in range(Q_CHUNKS):
                chain(half, i).wait_send()


def attend_and_project(queries, key_values, logit, out_weight, ctx_count, tp_count):
    width = out_weight.shape[1]
    vmem = pl.BlockSpec(memory_space=pltpu.VMEM)
    dma = pltpu.SemaphoreType.DMA
    return pl.pallas_call(
        functools.partial(attend_kernel, ctx_count, tp_count),
        out_shape=jax.ShapeDtypeStruct((ROWS, width), BF16),
        in_specs=[vmem, vmem, vmem, pl.BlockSpec(memory_space=pl.ANY)],
        out_specs=vmem,
        scratch_shapes=[
            pltpu.VMEM((2, Q_CHUNKS, WIDE, width), BF16),
            pltpu.VMEM((2, Q_CHUNKS, ROWS, WIDE), BF16),
            pltpu.VMEM((ROWS, width), F32),
            dma((2, Q_CHUNKS)),
            dma((2, Q_CHUNKS)),
            dma((2, Q_CHUNKS)),
        ],
        compiler_params=pltpu.CompilerParams(
            collective_id=1, has_side_effects=True, vmem_limit_bytes=52 * 2**20
        ),
        name="attend_and_project",
    )(queries, key_values, logit, out_weight)


def one_hot(index, count, axis):
    shape = (count,) + index.shape if axis == 0 else index.shape + (count,)
    iota = lax.broadcasted_iota(jnp.int32, shape, 0 if axis == 0 else len(shape) - 1)
    target = index[None] if axis == 0 else index[..., None]
    return (iota == target).astype(BF16)


def shards(hidden, norm_gain, router_weight, query_weight, key_value_weight, out_weight, kept_rows):
    me = lax.axis_index("ctx")
    ctx_count = lax.axis_size("ctx")
    tp_count = lax.axis_size("tp")
    token_count, width = hidden.shape
    capacity = kept_rows.shape[1]
    keep = capacity // 2
    part = capacity // ctx_count

    counts = jnp.sum((kept_rows < token_count).astype(jnp.int32), axis=1)
    starts = jnp.cumsum(counts) - counts
    ids = jnp.arange(ctx_count, dtype=jnp.int32)
    slots = jnp.arange(part, dtype=jnp.int32)

    first = (ids - starts[me]) % ctx_count
    send_index = first[:, None] + ctx_count * slots[None, :]
    own_rows = lax.dynamic_index_in_dim(kept_rows, me, 0, keepdims=False)
    send_rows = jnp.take(own_rows, send_index.reshape(-1), axis=0)
    pick = one_hot(send_rows, token_count, 1)
    sent = jnp.dot(pick, hidden, preferred_element_type=F32).astype(BF16)
    got = lax.all_to_all(sent.reshape(ctx_count, part, width), "ctx", 0, 0).reshape(capacity, width)

    come_first = (me - starts) % ctx_count
    come_slot = (starts + come_first)[:, None] // ctx_count + slots[None, :]
    come_valid = come_first[:, None] + ctx_count * slots[None, :] < counts[:, None]
    place = jnp.where(come_valid, come_slot, keep).reshape(-1)
    compact = one_hot(place, keep, 0)
    kept = jnp.dot(compact, got, preferred_element_type=F32).astype(BF16)

    widened = kept.astype(F32)
    square_part = jnp.sum(widened * widened, axis=1)
    router_part = jnp.dot(kept, router_weight, preferred_element_type=F32)
    normed = (widened * norm_gain.astype(F32)).astype(BF16)
    stats = jnp.pad(jnp.stack([square_part, router_part]), ((0, 6), (0, 0)))
    queries, key_values, logit = project(
        normed, stats, query_weight, key_value_weight, ctx_count, tp_count
    )
    row_update = attend_and_project(queries, key_values, logit, out_weight, ctx_count, tp_count)

    back = lax.dot_general(
        compact, row_update, (((0,), (0,)), ((), ())), preferred_element_type=F32
    ).astype(BF16)
    home = lax.all_to_all(back.reshape(ctx_count, part, width), "ctx", 0, 0).reshape(capacity, width)
    return lax.dot_general(
        pick, home, (((0,), (0,)), ((), ())), preferred_element_type=F32
    ).astype(BF16)


def solution(mesh):
    return jax.shard_map(
        shards,
        mesh=mesh,
        in_specs=(
            P("ctx", "tp"),
            P("tp"),
            P("tp"),
            P("tp", None),
            P(None, "tp", None),
            P(None, "tp"),
            P(),
        ),
        out_specs=P("ctx", "tp"),
        check_vma=False,
    )
```

time: 261 us -> 441 us (1.69)
  Pallas kernels: 8.82 us -> 358 us
  waiting for transfers between devices: 134 us -> 26.5 us
  matrix products: 35.4 us -> 13.3 us
  between operations: 13.3 us -> 0.08 us
  blocking collectives: 42.3 us -> 30.1 us
  local copies, waits for them, and re-layouts: 15.8 us -> 6.01 us
    pallas_call x1 -> x2, Pallas kernels: 8.82 us -> 358 us  [the longest x1 271 us: project(): pl.pallas_call(functools.partial(project_kernel, ctx_count, tp_count), ou...]
    all_gather x2 -> x0, waiting for transfers between devices: 69.1 us -> none  [the longest x1 46.1 us: shards(): gathered = lax.all_gather(head_output, 'tp', axis=0, tiled=False)]
    reduce_scatter x1 -> x0, waiting for transfers between devices: 38.4 us -> none  [shards(): sums = lax.psum_scatter(terms, 'tp', scatter_dimension=0, tiled=False)]
    psum x1 -> x0, blocking collectives: 12.3 us -> none  [shards(): square_sum, router_logit = lax.psum((square_part, router_part), 'tp')]
    dot_general x2 -> x0, matrix products: 11.8 us -> none  [the longest x1 8.41 us: shards(): lax.dot_general(query_weight, normed, (((0,), (1,)), ((), ())), preferred...]
    dot_general x1, matrix products: 11.4 us -> 0.76 us  [shards(): lax.dot_general(compact, row_update, (((0,), (0,)), ((), ())), preferred_...]
  transfers between devices with their start and end apart: 4 -> 1, of which waited for: 4 -> 1; matrix products, arithmetic and copies ran while one was open for 0% -> 0% of each run, Pallas kernels for 0% -> 0%
where the time goes in v2:
time: 441 us
  Pallas kernels  358 us (81%)
  blocking collectives  30.1 us (7%)
  waiting for transfers between devices  26.5 us (6%)
  matrix products  13.3 us (3%)
  local copies, waits for them, and re-layouts  6.01 us (1%)
  starting transfers between devices  5.3 us (1%)
    pallas_call x1, Pallas kernels, project(): pl.pallas_call(functools.partial(project_kernel, ctx_count, tp_count), ou...  271 us
    pallas_call x1, Pallas kernels, attend_and_project(): pl.pallas_call(functools.partial(attend_kernel, ctx_count, tp_count), out...  86.8 us
    all_to_all x1, blocking collectives, shards(): lax.all_to_all(back.reshape(ctx_count, part, width), 'ctx', 0, 0)  30.1 us
    all_to_all x1, waiting for transfers between devices, shards(): lax.all_to_all(sent.reshape(ctx_count, part, width), 'ctx', 0, 0)  26.5 us
  transfers between devices with their start and end apart: 1, of which 1 were waited for; matrix products, arithmetic and copies ran while one was open for 0% of the time, Pallas kernels for 0%

profile of v2, /device:TPU:0, one launch (start us, length us, event | category | flops | bytes accessed | tf_op | source)
XLA Modules:
  0.0 440.7 jit_solution(6878719598951552148)
XLA Ops:
  0.0 0.8 convert_reduce_fusion
  0.8 0.2 reduce-window.7
  1.0 0.7 constant_dynamic-slice_fusion
  1.8 0.6 dynamic_slice.7
  2.4 0.7 and_select_fusion.3
  3.0 0.1 add_select_fusion
  3.1 0.1 add.141
  3.2 0.1 add.138
  3.3 3.5 gather_fusion
  6.8 5.9 %convolution_convert_fusion.2 = bf16[512,2048]{1,0:T(8,128)(2,1)} fusion(bf16[1024,2048]{1,0:T(8,128)(2,1)} %param.7, s32[512]{0:T(512)S(1)} %and_select_fusion.2), kind=kOutput, calls=%fused_computation.3 | convolution fusion | flops 2149056512 | bytes 6293504 | tf_op jit(solution)/shard_map/dot_general | solution.py:346
  12.7 0.0 copy-start.1
  12.7 0.0 copy-start.2
  12.7 5.3 %all-to-all-start = ((bf16[8,64,2048]{2,1,0:T(8,128)(2,1)}), bf16[8,64,2048]{2,1,0:T(8,128)(2,1)S(1)}, u32[]{:S(2)}, u32[]{:S(2)}) async-start(bf16[8,64,2048]{2,1,0:T(8,128)(2,1)} %bitcast.22), calls=%async_computation | async-start | bytes 4194304 | tf_op jit(solution)/shard_map/all_to_all | solution.py:347
  18.0 0.1 select_n.83
  18.0 0.0 copy-done.1
  18.0 0.0 copy-done.2
  18.1 26.5 %all-to-all-done = bf16[8,64,2048]{2,1,0:T(8,128)(2,1)S(1)} async-done(((bf16[8,64,2048]{2,1,0:T(8,128)(2,1)}), bf16[8,64,2048]{2,1,0:T(8,128)(2,1)S(1)}, u32[]{:S(2)}, u32[]{:S(2)}) %all-to-all-start) | async-done | bytes 2097184 | tf_op jit(solution)/shard_map/all_to_all | solution.py:347
  44.6 1.8 fusion.1
  46.4 0.4 fusion.8
  46.8 270.9 %project_and_sum.1 = (bf16[8,256,256]{2,1,0:T(8,128)(2,1)S(1)}, bf16[8,2,256,256]{3,2,1,0:T(8,128)(2,1)}, f32[256,128]{1,0:T(8,128)S(1)}) custom-call(bf16[256,2048]{1,0:T(8,128)(2,1)} %get-tuple-element.15.x_ref, f32[8,256]{1,0:T(8,128)S(1)} %select_maximum_fusion.stats_ref, bf16[2048,4096]{1,0:T(8,128)(2,1)} %wq_ref.1, bf16[2,2048,512]{2,1,0:T(8,128)(2,1)} %wkv_ref.1), custom_call_target="tpu_custom_call" | custom-call | tf_op jit(solution)/shard_map/project_and_sum/pallas_call | solution.py:165
  317.6 0.0 copy-start
  317.7 1.0 copy-done
  318.6 86.8 %attend_and_project.1 = bf16[256,2048]{1,0:T(8,128)(2,1)S(1)} custom-call(bf16[8,256,256]{2,1,0:T(8,128)(2,1)} %copy-done, bf16[8,2,256,256]{3,2,1,0:T(8,128)(2,1)} %get-tuple-element.9.kv_ref, f32[256,128]{1,0:T(8,128)S(1)} %get-tuple-element.10.logit_ref, bf16[4096,2048]{1,0:T(8,128)(2,1)} %wo_ref.1), custom_call_target="tpu_custom_call" | custom-call | tf_op jit(solution)/shard_map/attend_and_project/pallas_call | solution.py:300
  405.4 0.8 convolution_convert_fusion.1
  406.1 30.1 %all_to_all.10 = bf16[8,64,2048]{2,1,0:T(8,128)(2,1)S(1)} all-to-all(bf16[8,64,2048]{2,1,0:T(8,128)(2,1)S(1)} %bitcast.20), channel_id=1, replica_groups=mesh['ctx'=8,'tp'=4] {'ctx'}, dimensions={0} | all-to-all | bytes 4194304 | tf_op jit(solution)/shard_map/all_to_all | solution.py:369
  436.2 4.5 %convolution_convert_fusion = bf16[1024,2048]{1,0:T(8,128)(2,1)} fusion(bf16[512,2048]{1,0:T(8,128)(2,1)S(1)} %bitcast.23, s32[512]{0:T(512)S(1)} %and_select_fusion.2), kind=kOutput, calls=%fused_computation.1 | convolution fusion | flops 2150105088 | bytes 6293504 | tf_op jit(solution)/shard_map/dot_general | solution.py:370
  (8 shorter events, 0.1 us)
Async XLA Ops:
  12.7 5.4 %copy-start.1 = (bf16[2048]{0:T(1024)(128)(2,1)S(1)}, bf16[2048]{0:T(1024)(128)(2,1)}, u32[]{:S(2)}) copy-start(bf16[2048]{0:T(1024)(128)(2,1)} %param.8) | copy-start | bytes 12292
  12.7 5.4 %copy-start.2 = (bf16[2048]{0:T(1024)(128)(2,1)S(1)}, bf16[2048]{0:T(1024)(128)(2,1)}, u32[]{:S(2)}) copy-start(bf16[2048]{0:T(1024)(128)(2,1)} %param.9) | copy-start | bytes 12292
  12.7 31.9 %all-to-all-start = ((bf16[8,64,2048]{2,1,0:T(8,128)(2,1)}), bf16[8,64,2048]{2,1,0:T(8,128)(2,1)S(1)}, u32[]{:S(2)}, u32[]{:S(2)}) async-start(bf16[8,64,2048]{2,1,0:T(8,128)(2,1)} %bitcast.22), calls=%async_computation | async-start | bytes 4194304 | tf_op jit(solution)/shard_map/all_to_all | solution.py:347
  317.6 1.0 copy-start

commit v3 on v1

--- a/solution.py
+++ b/solution.py
@@ -103,31 +103,52 @@
     square_part = jnp.sum(widened * widened, axis=1)
     router_part = jnp.dot(kept, router_weight, preferred_element_type=F32)
     normed = (widened * norm_gain.astype(F32)).astype(BF16)
-    square_sum, router_logit = lax.psum((square_part, router_part), "tp")
-    inverse_rms = lax.rsqrt(square_sum / D + EPSILON)
 
-    q_terms = lax.dot_general(
-        query_weight, normed, (((0,), (1,)), ((), ())), preferred_element_type=F32
-    ).astype(BF16).reshape(tp_count, heads * HD, keep)
+    pieces = []
+    remainder = jnp.stack([square_part, router_part])
+    for _ in range(3):
+        piece = lax.reduce_precision(remainder, 8, 7)
+        pieces.append(piece.astype(BF16))
+        remainder = remainder - piece
+    own_slot = (jnp.arange(tp_count) == tp_index)[:, None, None]
+    stat_terms = jnp.where(own_slot, jnp.concatenate(pieces)[None], 0).reshape(6 * tp_count, keep)
+    stat_terms = jnp.broadcast_to(stat_terms[None], (tp_count,) + stat_terms.shape)
+
     kv_terms = lax.dot_general(
         key_value_weight, normed, (((1,), (1,)), ((), ())), preferred_element_type=F32
     ).astype(BF16).reshape(2, KVH, HD, keep)
     group_of = [t * heads // (H // KVH) for t in range(tp_count)]
     kv_terms = jnp.stack([kv_terms[:, g] for g in group_of]).reshape(tp_count, 2 * HD, keep)
-    terms = jnp.concatenate([q_terms, kv_terms], axis=1)
-    sums = lax.psum_scatter(terms, "tp", scatter_dimension=0, tiled=False)
-    scaled = (sums.astype(F32) * inverse_rms[None, :]).astype(BF16).T
-    queries = scaled[:, : heads * HD]
-    key_values = lax.all_gather(scaled[:, heads * HD :], "ctx", axis=0, tiled=False)
-    head_output = attention(
-        queries, key_values[:, :, :HD], key_values[:, :, HD:], me.reshape(1), ctx_count, keep
+    kv_sums = lax.psum_scatter(
+        jnp.concatenate([kv_terms, stat_terms], axis=1), "tp", scatter_dimension=0, tiled=False
     )
+    q_terms = lax.dot_general(
+        query_weight, normed, (((0,), (1,)), ((), ())), preferred_element_type=F32
+    ).astype(BF16)
+    q_sums = lax.psum_scatter(q_terms, "tp", scatter_dimension=0, tiled=True)
 
-    gathered = lax.all_gather(head_output, "tp", axis=0, tiled=False)
-    projected = jnp.einsum(
-        "tqe,tef->qf", gathered, out_weight.reshape(tp_count, heads * HD, width),
-        preferred_element_type=F32,
+    stats = jnp.sum(kv_sums[2 * HD :].astype(F32).reshape(tp_count * 3, 2, keep), axis=0)
+    inverse_rms = lax.rsqrt(stats[0] / D + EPSILON)
+    router_logit = stats[1]
+    key_values = (kv_sums[: 2 * HD].astype(F32) * inverse_rms[None, :]).astype(BF16).T
+    key_values = lax.all_to_all(
+        jnp.broadcast_to(key_values[None], (ctx_count,) + key_values.shape), "ctx", 0, 0
     )
+    queries = (q_sums.astype(F32) * inverse_rms[None, :]).astype(BF16).T
+
+    batches = 2
+    size = heads // batches * HD
+    weight = out_weight.reshape(tp_count, batches, size, width)
+    projected = 0.0
+    for b in range(batches):
+        head_output = attention(
+            queries[:, b * size : (b + 1) * size], key_values[:, :, :HD], key_values[:, :, HD:],
+            me.reshape(1), ctx_count, keep,
+        )
+        gathered = lax.all_gather(head_output, "tp", axis=0, tiled=False)
+        projected = projected + jnp.einsum(
+            "tqe,tef->qf", gathered, weight[:, b], preferred_element_type=F32
+        )
     row_update = (jax.nn.sigmoid(router_logit)[:, None] * projected).astype(BF16)
 
     back = lax.dot_general(

time: 261 us -> 236 us (0.904)
  waiting for transfers between devices: 134 us -> 104 us
  local copies, waits for them, and re-layouts: 15.8 us -> 7.14 us
  blocking collectives: 42.3 us -> 48.9 us
  matrix products: 35.4 us -> 41.2 us
    all_gather x1 -> x0, waiting for transfers between devices: 23 us -> none  [shards(): lax.all_gather(scaled[:, heads * HD:], 'ctx', axis=0, tiled=False)]
    all_to_all x0 -> x1, blocking collectives: none -> 18.8 us  [shards(): lax.all_to_all(jnp.broadcast_to(key_values[None], (ctx_count,) + key_valu...]
    psum x1 -> x0, blocking collectives: 12.3 us -> none  [shards(): square_sum, router_logit = lax.psum((square_part, router_part), 'tp')]
    dot_general x0 -> x1, matrix products: none -> 7.37 us  [shards(): jnp.einsum('tqe,tef->qf', gathered, weight[:, b], preferred_element_type=...]
    reduce_scatter x1 -> x2, waiting for transfers between devices: 38.4 us -> 33.4 us  [the longest x1 23.6 us: shards(): q_sums = lax.psum_scatter(q_terms, 'tp', scatter_dimension=0, tiled=True)]
    dot_general x1, matrix products: 11.4 us -> 7.2 us  [shards(): lax.dot_general(compact, row_update, (((0,), (0,)), ((), ())), preferred_...]
    dot_general x1, matrix products: 8.41 us -> 11.5 us  [shards(): lax.dot_general(query_weight, normed, (((0,), (1,)), ((), ())), preferred...]
    reshape x1 -> x0, local copies, waits for them, and re-layouts: 2.99 us -> none  [shards(): q_terms = lax.dot_general(query_weight, normed, (((0,), (1,)), ((), ())),...]
  transfers between devices with their start and end apart: 4 -> 5, of which waited for: 4 -> 5; matrix products, arithmetic and copies ran while one was open for 0% -> 9% of each run, Pallas kernels for 0% -> 2%
where the time goes in v3:
time: 236 us; the launch traced here: 235 us
  waiting for transfers between devices  104 us (44%)
  blocking collectives  48.9 us (21%)
  matrix products  41.2 us (17%)
  between operations  13.3 us (6%)
  Pallas kernels  9.8 us (4%)
  local copies, waits for them, and re-layouts  7.14 us (3%)
  other arithmetic  5.64 us (2%)
  starting transfers between devices  5.46 us (2%)
    all_gather x2, waiting for transfers between devices, shards(): gathered = lax.all_gather(head_output, 'tp', axis=0, tiled=False)  44 us
    all_to_all x1, blocking collectives, shards(): lax.all_to_all(back.reshape(ctx_count, part, width), 'ctx', 0, 0)  30.1 us
    all_to_all x1, waiting for transfers between devices, shards(): lax.all_to_all(sent.reshape(ctx_count, part, width), 'ctx', 0, 0)  26.3 us
    reduce_scatter x1, waiting for transfers between devices, shards(): q_sums = lax.psum_scatter(q_terms, 'tp', scatter_dimension=0, tiled=True)  23.6 us
    all_to_all x1, blocking collectives, shards(): lax.all_to_all(jnp.broadcast_to(key_values[None], (ctx_count,) + key_valu...  18.8 us
    dot_general x1, matrix products, shards(): lax.dot_general(query_weight, normed, (((0,), (1,)), ((), ())), preferred...  11.5 us
    reduce_scatter x1, waiting for transfers between devices, shards(): lax.psum_scatter(jnp.concatenate([kv_terms, stat_terms], axis=1), 'tp', s...  9.88 us
    pallas_call x2, Pallas kernels, attention(): pl.pallas_call(functools.partial(attention_kernel, ctx_count, keep), out_...  9.8 us
  transfers between devices with their start and end apart: 5, of which 5 were waited for; matrix products, arithmetic and copies ran while one was open for 9% of the time, Pallas kernels for 2%

profile of v3, /device:TPU:0, one launch (start us, length us, event | category | flops | bytes accessed | tf_op | source)
XLA Modules:
  0.0 235.3 jit_solution(9684730852942368096)
XLA Ops:
  6.5 0.8 convert_reduce_fusion
  7.4 0.2 reduce-window.7
  7.6 0.7 constant_dynamic-slice_fusion
  8.3 0.6 dynamic_slice.7
  8.9 0.7 and_select_fusion.3
  9.6 0.1 add_select_fusion
  9.6 0.1 add.161
  9.7 0.1 add.158
  9.8 3.5 %gather_fusion = s32[512]{0:T(512)S(1)} fusion(s32[512]{0:T(512)S(1)} %bitcast.80, s32[1024]{0:T(1024)S(1)} %pad_clamp_fusion), kind=kCustom, calls=%fused_computation | custom fusion | bytes 6144 | tf_op jit(solution)/shard_map/jit(_take)/gather | solution.py:90
  13.3 5.9 %convolution_convert_fusion.3 = bf16[512,2048]{1,0:T(8,128)(2,1)} fusion(bf16[1024,2048]{1,0:T(8,128)(2,1)} %param.7, s32[512]{0:T(512)S(1)} %and_select_fusion.2), kind=kOutput, calls=%fused_computation.9 | convolution fusion | flops 2149056512 | bytes 6293504 | tf_op jit(solution)/shard_map/dot_general | solution.py:92
  19.2 0.0 copy-start
  19.2 0.0 copy-start.1
  19.2 5.3 %all-to-all-start = ((bf16[8,64,2048]{2,1,0:T(8,128)(2,1)}), bf16[8,64,2048]{2,1,0:T(8,128)(2,1)S(1)}, u32[]{:S(2)}, u32[]{:S(2)}) async-start(bf16[8,64,2048]{2,1,0:T(8,128)(2,1)} %bitcast.82), calls=%async_computation | async-start | bytes 4194304 | tf_op jit(solution)/shard_map/all_to_all | solution.py:93
  24.5 0.0 reduce-scatter.3.cloned.1.call-start
  24.6 0.1 broadcast_in_dim.63
  24.6 0.1 broadcast_in_dim.64
  24.7 0.1 select_n.91
  24.8 0.0 copy-done
  24.8 0.0 copy-done.1
  24.8 26.3 %all-to-all-done = bf16[8,64,2048]{2,1,0:T(8,128)(2,1)S(1)} async-done(((bf16[8,64,2048]{2,1,0:T(8,128)(2,1)}), bf16[8,64,2048]{2,1,0:T(8,128)(2,1)S(1)}, u32[]{:S(2)}, u32[]{:S(2)}) %all-to-all-start) | async-done | bytes 2097184 | tf_op jit(solution)/shard_map/all_to_all | solution.py:93
  51.1 0.8 fusion.9
  52.0 0.4 fusion.33
  52.4 3.4 %fusion.10 = bf16[2,512,256]{1,2,0:T(8,128)(2,1)S(1)} fusion(bf16[2,2048,512]{2,1,0:T(8,128)(2,1)} %param.11, bf16[256,2048]{1,0:T(8,128)(2,1)S(1)} %get-tuple-element.24, f32[2048]{0:T(1024)S(1)} %convert_element_type.82), kind=kOutput, calls=%fused_computation.22 | convolution fusion | flops 1075576832 | bytes 5775360 | tf_op jit(solution)/shard_map/dot_general | solution.py:117
  55.9 0.1 reshape.259
  56.0 0.8 fusion.32
  56.8 0.1 copy.12
  56.9 0.1 copy.15
  57.1 0.1 copy.14
  57.2 0.1 copy.13
  57.3 0.1 broadcast_select_fusion
  57.4 0.9 pad_maximum_fusion
  58.3 0.0 reduce-scatter.3.cloned.1.call-update
  58.3 0.0 reduce-scatter.5.cloned.1.call-start
  58.3 11.5 %fusion.2 = bf16[4096,256]{0,1:T(8,128)(2,1)} fusion(bf16[2048,4096]{1,0:T(8,128)(2,1)} %param.10, bf16[256,2048]{1,0:T(8,128)(2,1)S(1)} %get-tuple-element.24, f32[2048]{0:T(1024)S(1)} %convert_element_type.82), kind=kOutput, calls=%fused_computation.6 | convolution fusion | flops 4297588736 | bytes 19931136 | tf_op jit(solution)/shard_map/dot_general | solution.py:125
  69.9 0.0 reduce-scatter.5.cloned.1.call-update
  69.9 0.0 all-gather.5.cloned.1.call-start
  70.0 9.9 %reduce-scatter.3.cloned.1.call-done = bf16[1,280,256]{2,1,0:T(8,128)(2,1)} async-done(((bf16[4,280,256]{2,1,0:T(8,128)(2,1)}), bf16[1,280,256]{2,1,0:T(8,128)(2,1)}) %reduce-scatter.3.cloned.1.call-update) | async-done | bytes 143376 | tf_op jit(solution)/shard_map/reduce_scatter | solution.py:122
  79.9 0.7 slice_convert_fusion
  80.6 0.9 fusion.20
  81.6 0.1 copy.16
  81.7 0.1 broadcast_in_dim.70
  81.8 18.8 %all_to_all.15 = bf16[8,256,256]{2,1,0:T(8,128)(2,1)S(1)} all-to-all(bf16[8,256,256]{2,1,0:T(8,128)(2,1)S(1)} %broadcast_in_dim.70), channel_id=1, replica_groups=mesh['ctx'=8,'tp'=4] {'ctx'}, dimensions={0} | all-to-all | bytes 2097152 | tf_op jit(solution)/shard_map/all_to_all | solution.py:134
  100.6 0.3 fusion.30
  100.9 23.6 %reduce-scatter.5.cloned.1.call-done = bf16[1024,256]{0,1:T(8,128)(2,1)} async-done(((bf16[4096,256]{0,1:T(8,128)(2,1)}), bf16[1024,256]{0,1:T(8,128)(2,1)}) %reduce-scatter.5.cloned.1.call-update) | async-done | bytes 524304 | tf_op jit(solution)/shard_map/reduce_scatter | solution.py:128
  124.4 1.2 fusion.16
  125.7 4.9 %attention.2 = bf16[256,512]{1,0:T(8,128)(2,1)} custom-call(bf16[256,512]{1,0:T(8,128)(2,1)S(1)} %get-tuple-element.11.q_ref, bf16[8,256,128]{2,1,0:T(8,128)(2,1)S(1)} %get-tuple-element.9.k_ref, bf16[8,256,128]{2,1,0:T(8,128)(2,1)S(1)} %get-tuple-element.8.v_ref, s32[1]{0:T(128)} %bitcast.21.me_ref), custom_call_target="tpu_custom_call" | custom-call | tf_op jit(solution)/shard_map/attention/pallas_call | solution.py:53
  130.6 0.0 all-gather.5.cloned.1.call-update
  130.6 0.0 all-gather.7.cloned.1.call-start
  130.6 4.9 %attention.3 = bf16[256,512]{1,0:T(8,128)(2,1)} custom-call(bf16[256,512]{1,0:T(8,128)(2,1)S(1)} %get-tuple-element.10.q_ref, bf16[8,256,128]{2,1,0:T(8,128)(2,1)S(1)} %get-tuple-element.9.k_ref, bf16[8,256,128]{2,1,0:T(8,128)(2,1)S(1)} %get-tuple-element.8.v_ref, s32[1]{0:T(128)} %bitcast.21.me_ref), custom_call_target="tpu_custom_call" | custom-call | tf_op jit(solution)/shard_map/attention/pallas_call | solution.py:53
  135.5 0.0 all-gather.7.cloned.1.call-update
  135.5 22.4 %all-gather.5.cloned.1.call-done = bf16[1024,512]{1,0:T(8,128)(2,1)} async-done(((bf16[256,512]{1,0:T(8,128)(2,1)}), bf16[1024,512]{1,0:T(8,128)(2,1)}) %all-gather.5.cloned.1.call-update) | async-done | bytes 1048592 | tf_op jit(solution)/shard_map/all_gather | solution.py:148
  158.0 7.4 %fusion.3 = f32[256,2048]{1,0:T(8,128)} fusion(bf16[4,256,512]{2,1,0:T(8,128)(2,1)} %bitcast.97, bf16[4,2,512,2048]{3,2,1,0:T(8,128)(2,1)} %bitcast.95), kind=kOutput, calls=%fused_computation.10 | convolution fusion | flops 2147483648 | bytes 11534336 | tf_op jit(solution)/shard_map/tqe,tef->qf/dot_general | solution.py:149
  165.4 21.6 %all-gather.7.cloned.1.call-done = bf16[1024,512]{1,0:T(8,128)(2,1)} async-done(((bf16[256,512]{1,0:T(8,128)(2,1)}), bf16[1024,512]{1,0:T(8,128)(2,1)}) %all-gather.7.cloned.1.call-update) | async-done | bytes 1048592 | tf_op jit(solution)/shard_map/all_gather | solution.py:148
  187.0 7.2 %convolution_convert_fusion.2 = bf16[512,2048]{1,0:T(8,128)(2,1)S(1)} fusion(f32[256,2048]{1,0:T(8,128)} %fusion.3, bf16[4,256,512]{2,1,0:T(8,128)(2,1)} %bitcast.98, bf16[4,2,512,2048]{3,2,1,0:T(8,128)(2,1)} %bitcast.96, f32[256]{0:T(256)S(1)} %bitcast.94, s32[512]{0:T(512)S(1)} %select_n.91), kind=kOutput, calls=%fused_computation.8 | convolution fusion | flops 2687107072 | bytes 13634560 | tf_op jit(solution)/shard_map/dot_general | solution.py:154
  194.2 30.1 %all_to_all.16 = bf16[8,64,2048]{2,1,0:T(8,128)(2,1)S(1)} all-to-all(bf16[8,64,2048]{2,1,0:T(8,128)(2,1)S(1)} %bitcast.83), channel_id=1, replica_groups=mesh['ctx'=8,'tp'=4] {'ctx'}, dimensions={0} | all-to-all | bytes 4194304 | tf_op jit(solution)/shard_map/all_to_all | solution.py:157
  224.2 4.5 %convolution_convert_fusion.1 = bf16[1024,2048]{1,0:T(8,128)(2,1)} fusion(bf16[512,2048]{1,0:T(8,128)(2,1)S(1)} %bitcast.84, s32[512]{0:T(512)S(1)} %and_select_fusion.2), kind=kOutput, calls=%fused_computation.7 | convolution fusion | flops 2150105088 | bytes 6293504 | tf_op jit(solution)/shard_map/dot_general | solution.py:158
  (17 shorter events, 0.2 us)
Async XLA Ops:
  19.2 5.6 %copy-start = (bf16[2048]{0:T(1024)(128)(2,1)S(1)}, bf16[2048]{0:T(1024)(128)(2,1)}, u32[]{:S(2)}) copy-start(bf16[2048]{0:T(1024)(128)(2,1)} %param.8) | copy-start | bytes 12292
  19.2 5.6 %copy-start.1 = (bf16[2048]{0:T(1024)(128)(2,1)S(1)}, bf16[2048]{0:T(1024)(128)(2,1)}, u32[]{:S(2)}) copy-start(bf16[2048]{0:T(1024)(128)(2,1)} %param.9) | copy-start | bytes 12292
  19.2 31.9 %all-to-all-start = ((bf16[8,64,2048]{2,1,0:T(8,128)(2,1)}), bf16[8,64,2048]{2,1,0:T(8,128)(2,1)S(1)}, u32[]{:S(2)}, u32[]{:S(2)}) async-start(bf16[8,64,2048]{2,1,0:T(8,128)(2,1)} %bitcast.82), calls=%async_computation | async-start | bytes 4194304 | tf_op jit(solution)/shard_map/all_to_all | solution.py:93
  24.5 55.4 %reduce-scatter.3.cloned.1.call-start = ((), (), s32[]{:S(2)}) async-start(), calls=%async_computation.5 | async-start | bytes 716800 | tf_op jit(solution)/shard_map/reduce_scatter | solution.py:122
  58.3 66.1 %reduce-scatter.5.cloned.1.call-start = ((), (), s32[]{:S(2)}) async-start(), calls=%async_computation.6 | async-start | bytes 2621440 | tf_op jit(solution)/shard_map/reduce_scatter | solution.py:128
  69.9 88.1 %all-gather.5.cloned.1.call-start = ((), (), s32[]{:S(2)}) async-start(), calls=%async_computation.7 | async-start | bytes 1310720 | tf_op jit(solution)/shard_map/all_gather | solution.py:148
  130.6 56.4 %all-gather.7.cloned.1.call-start = ((), (), s32[]{:S(2)}) async-start(), calls=%async_computation.8 | async-start | bytes 1310720 | tf_op jit(solution)/shard_map/all_gather | solution.py:148
Sparse Core Ops, SparseCore 0:
  58.4 21.3 reduce-scatter.2
  82.1 42.2 reduce-scatter.4
  130.7 27.2 all-gather.4
  159.5 27.4 all-gather.6

commit v4 on v3

--- a/solution.py
+++ b/solution.py
@@ -87,7 +87,8 @@
     first = (ids - starts[me]) % ctx_count
     send_index = first[:, None] + ctx_count * slots[None, :]
     own_rows = lax.dynamic_index_in_dim(kept_rows, me, 0, keepdims=False)
-    send_rows = jnp.take(own_rows, send_index.reshape(-1), axis=0)
+    hits = send_index.reshape(-1)[:, None] == jnp.arange(capacity, dtype=jnp.int32)[None, :]
+    send_rows = jnp.sum(jnp.where(hits, own_rows[None, :], 0), axis=1)
     pick = one_hot(send_rows, token_count, 1)
     sent = jnp.dot(pick, hidden, preferred_element_type=F32).astype(BF16)
     got = lax.all_to_all(sent.reshape(ctx_count, part, width), "ctx", 0, 0).reshape(capacity, width)

time: 236 us -> 233 us (0.987)
  local copies, waits for them, and re-layouts: 7.14 us -> 3.58 us
    gather x1 -> x0, local copies, waits for them, and re-layouts: 3.49 us -> none  [shards(): send_rows = jnp.take(own_rows, send_index.reshape(-1), axis=0)]
where the time goes in v4:
time: 233 us; the launch traced here: 232 us
  waiting for transfers between devices  104 us (45%)
  blocking collectives  48.8 us (21%)
  matrix products  41.2 us (18%)
  between operations  13.3 us (6%)
  Pallas kernels  9.83 us (4%)
  other arithmetic  5.86 us (3%)
  starting transfers between devices  5.47 us (2%)
  local copies, waits for them, and re-layouts  3.58 us (2%)
    all_gather x2, waiting for transfers between devices, shards(): gathered = lax.all_gather(head_output, 'tp', axis=0, tiled=False)  44 us
    all_to_all x1, blocking collectives, shards(): lax.all_to_all(back.reshape(ctx_count, part, width), 'ctx', 0, 0)  30.1 us
    all_to_all x1, waiting for transfers between devices, shards(): lax.all_to_all(sent.reshape(ctx_count, part, width), 'ctx', 0, 0)  26.3 us
    reduce_scatter x1, waiting for transfers between devices, shards(): q_sums = lax.psum_scatter(q_terms, 'tp', scatter_dimension=0, tiled=True)  23.6 us
    all_to_all x1, blocking collectives, shards(): lax.all_to_all(jnp.broadcast_to(key_values[None], (ctx_count,) + key_valu...  18.8 us
    dot_general x1, matrix products, shards(): lax.dot_general(query_weight, normed, (((0,), (1,)), ((), ())), preferred...  11.5 us
    reduce_scatter x1, waiting for transfers between devices, shards(): lax.psum_scatter(jnp.concatenate([kv_terms, stat_terms], axis=1), 'tp', s...  9.91 us
    pallas_call x2, Pallas kernels, attention(): pl.pallas_call(functools.partial(attention_kernel, ctx_count, keep), out_...  9.83 us
  transfers between devices with their start and end apart: 5, of which 5 were waited for; matrix products, arithmetic and copies ran while one was open for 9% of the time, Pallas kernels for 2%

profile of v4, /device:TPU:0, one launch (start us, length us, event | category | flops | bytes accessed | tf_op | source)
XLA Modules:
  0.0 231.9 jit_solution(6686939971398748345)
XLA Ops:
  6.5 0.8 convert_reduce_fusion
  7.4 0.2 reduce-window.7
  7.6 0.7 constant_dynamic-slice_fusion
  8.3 0.6 dynamic_slice.7
  8.9 0.7 and_select_fusion.2
  9.6 0.1 add_select_fusion
  9.6 0.1 add.122
  9.7 0.3 select_reduce_fusion
  10.0 5.9 %convolution_convert_fusion.3 = bf16[512,2048]{1,0:T(8,128)(2,1)} fusion(bf16[1024,2048]{1,0:T(8,128)(2,1)} %param.7, s32[512]{0:T(512)S(1)} %select_reduce_fusion), kind=kOutput, calls=%fused_computation.8 | convolution fusion | flops 2149056512 | bytes 6293504 | tf_op jit(solution)/shard_map/dot_general | solution.py:93
  15.8 0.0 copy-start
  15.8 0.0 copy-start.1
  15.8 5.3 %all-to-all-start = ((bf16[8,64,2048]{2,1,0:T(8,128)(2,1)}), bf16[8,64,2048]{2,1,0:T(8,128)(2,1)S(1)}, u32[]{:S(2)}, u32[]{:S(2)}) async-start(bf16[8,64,2048]{2,1,0:T(8,128)(2,1)} %bitcast.84), calls=%async_computation | async-start | bytes 4194304 | tf_op jit(solution)/shard_map/all_to_all | solution.py:94
  21.2 0.0 reduce-scatter.3.cloned.1.call-start
  21.2 0.1 broadcast_in_dim.75
  21.3 0.1 broadcast_in_dim.76
  21.4 0.1 select_n.66
  21.5 0.0 copy-done
  21.5 0.0 copy-done.1
  21.5 26.3 %all-to-all-done = bf16[8,64,2048]{2,1,0:T(8,128)(2,1)S(1)} async-done(((bf16[8,64,2048]{2,1,0:T(8,128)(2,1)}), bf16[8,64,2048]{2,1,0:T(8,128)(2,1)S(1)}, u32[]{:S(2)}, u32[]{:S(2)}) %all-to-all-start) | async-done | bytes 2097184 | tf_op jit(solution)/shard_map/all_to_all | solution.py:94
  47.8 0.8 fusion.9
  48.6 0.4 fusion.33
  49.1 3.4 %fusion.10 = bf16[2,512,256]{1,2,0:T(8,128)(2,1)S(1)} fusion(bf16[2,2048,512]{2,1,0:T(8,128)(2,1)} %param.11, bf16[256,2048]{1,0:T(8,128)(2,1)S(1)} %get-tuple-element.24, f32[2048]{0:T(1024)S(1)} %convert_element_type.82), kind=kOutput, calls=%fused_computation.21 | convolution fusion | flops 1075576832 | bytes 5775360 | tf_op jit(solution)/shard_map/dot_general | solution.py:118
  52.5 0.1 reshape.223
  52.7 0.8 fusion.32
  53.4 0.1 copy.22
  53.6 0.1 copy.25
  53.7 0.1 copy.24
  53.9 0.1 copy.23
  54.0 0.1 broadcast_select_fusion
  54.1 0.8 pad_maximum_fusion
  54.9 0.0 reduce-scatter.3.cloned.1.call-update
  54.9 0.0 reduce-scatter.5.cloned.1.call-start
  55.0 11.5 %fusion.2 = bf16[4096,256]{0,1:T(8,128)(2,1)} fusion(bf16[2048,4096]{1,0:T(8,128)(2,1)} %param.10, bf16[256,2048]{1,0:T(8,128)(2,1)S(1)} %get-tuple-element.24, f32[2048]{0:T(1024)S(1)} %convert_element_type.82), kind=kOutput, calls=%fused_computation.5 | convolution fusion | flops 4297588736 | bytes 19931136 | tf_op jit(solution)/shard_map/dot_general | solution.py:126
  66.5 0.0 reduce-scatter.5.cloned.1.call-update
  66.6 0.0 all-gather.5.cloned.1.call-start
  66.6 9.9 %reduce-scatter.3.cloned.1.call-done = bf16[1,280,256]{2,1,0:T(8,128)(2,1)} async-done(((bf16[4,280,256]{2,1,0:T(8,128)(2,1)}), bf16[1,280,256]{2,1,0:T(8,128)(2,1)}) %reduce-scatter.3.cloned.1.call-update) | async-done | bytes 143376 | tf_op jit(solution)/shard_map/reduce_scatter | solution.py:123
  76.5 0.7 slice_convert_fusion
  77.3 0.9 fusion.20
  78.2 0.1 copy.26
  78.4 0.1 broadcast_in_dim.82
  78.4 18.8 %all_to_all.15 = bf16[8,256,256]{2,1,0:T(8,128)(2,1)S(1)} all-to-all(bf16[8,256,256]{2,1,0:T(8,128)(2,1)S(1)} %broadcast_in_dim.82), channel_id=1, replica_groups=mesh['ctx'=8,'tp'=4] {'ctx'}, dimensions={0} | all-to-all | bytes 2097152 | tf_op jit(solution)/shard_map/all_to_all | solution.py:135
  97.2 0.3 fusion.30
  97.5 23.6 %reduce-scatter.5.cloned.1.call-done = bf16[1024,256]{0,1:T(8,128)(2,1)} async-done(((bf16[4096,256]{0,1:T(8,128)(2,1)}), bf16[1024,256]{0,1:T(8,128)(2,1)}) %reduce-scatter.5.cloned.1.call-update) | async-done | bytes 524304 | tf_op jit(solution)/shard_map/reduce_scatter | solution.py:129
  121.0 1.2 fusion.16
  122.3 4.9 %attention.2 = bf16[256,512]{1,0:T(8,128)(2,1)} custom-call(bf16[256,512]{1,0:T(8,128)(2,1)S(1)} %get-tuple-element.11.q_ref, bf16[8,256,128]{2,1,0:T(8,128)(2,1)S(1)} %get-tuple-element.9.k_ref, bf16[8,256,128]{2,1,0:T(8,128)(2,1)S(1)} %get-tuple-element.8.v_ref, s32[1]{0:T(128)} %bitcast.20.me_ref), custom_call_target="tpu_custom_call" | custom-call | tf_op jit(solution)/shard_map/attention/pallas_call | solution.py:53
  127.2 0.0 all-gather.5.cloned.1.call-update
  127.2 0.0 all-gather.7.cloned.1.call-start
  127.3 4.9 %attention.3 = bf16[256,512]{1,0:T(8,128)(2,1)} custom-call(bf16[256,512]{1,0:T(8,128)(2,1)S(1)} %get-tuple-element.10.q_ref, bf16[8,256,128]{2,1,0:T(8,128)(2,1)S(1)} %get-tuple-element.9.k_ref, bf16[8,256,128]{2,1,0:T(8,128)(2,1)S(1)} %get-tuple-element.8.v_ref, s32[1]{0:T(128)} %bitcast.20.me_ref), custom_call_target="tpu_custom_call" | custom-call | tf_op jit(solution)/shard_map/attention/pallas_call | solution.py:53
  132.2 0.0 all-gather.7.cloned.1.call-update
  132.2 22.4 %all-gather.5.cloned.1.call-done = bf16[1024,512]{1,0:T(8,128)(2,1)} async-done(((bf16[256,512]{1,0:T(8,128)(2,1)}), bf16[1024,512]{1,0:T(8,128)(2,1)}) %all-gather.5.cloned.1.call-update) | async-done | bytes 1048592 | tf_op jit(solution)/shard_map/all_gather | solution.py:149
  154.6 7.4 %fusion.3 = f32[256,2048]{1,0:T(8,128)} fusion(bf16[4,256,512]{2,1,0:T(8,128)(2,1)} %bitcast.99, bf16[4,2,512,2048]{3,2,1,0:T(8,128)(2,1)} %bitcast.97), kind=kOutput, calls=%fused_computation.9 | convolution fusion | flops 2147483648 | bytes 11534336 | tf_op jit(solution)/shard_map/tqe,tef->qf/dot_general | solution.py:150
  162.0 21.6 %all-gather.7.cloned.1.call-done = bf16[1024,512]{1,0:T(8,128)(2,1)} async-done(((bf16[256,512]{1,0:T(8,128)(2,1)}), bf16[1024,512]{1,0:T(8,128)(2,1)}) %all-gather.7.cloned.1.call-update) | async-done | bytes 1048592 | tf_op jit(solution)/shard_map/all_gather | solution.py:149
  183.6 7.2 %convolution_convert_fusion.2 = bf16[512,2048]{1,0:T(8,128)(2,1)S(1)} fusion(f32[256,2048]{1,0:T(8,128)} %fusion.3, bf16[4,256,512]{2,1,0:T(8,128)(2,1)} %bitcast.100, bf16[4,2,512,2048]{3,2,1,0:T(8,128)(2,1)} %bitcast.98, f32[256]{0:T(256)S(1)} %bitcast.96, s32[512]{0:T(512)S(1)} %select_n.66), kind=kOutput, calls=%fused_computation.7 | convolution fusion | flops 2687107072 | bytes 13634560 | tf_op jit(solution)/shard_map/dot_general | solution.py:155
  190.8 30.1 %all_to_all.16 = bf16[8,64,2048]{2,1,0:T(8,128)(2,1)S(1)} all-to-all(bf16[8,64,2048]{2,1,0:T(8,128)(2,1)S(1)} %bitcast.85), channel_id=1, replica_groups=mesh['ctx'=8,'tp'=4] {'ctx'}, dimensions={0} | all-to-all | bytes 4194304 | tf_op jit(solution)/shard_map/all_to_all | solution.py:158
  220.8 4.5 %convolution_convert_fusion.1 = bf16[1024,2048]{1,0:T(8,128)(2,1)} fusion(bf16[512,2048]{1,0:T(8,128)(2,1)S(1)} %bitcast.86, s32[512]{0:T(512)S(1)} %select_reduce_fusion), kind=kOutput, calls=%fused_computation.6 | convolution fusion | flops 2150105088 | bytes 6293504 | tf_op jit(solution)/shard_map/dot_general | solution.py:159
  (14 shorter events, 0.2 us)
Async XLA Ops:
  15.8 5.6 %copy-start = (bf16[2048]{0:T(1024)(128)(2,1)S(1)}, bf16[2048]{0:T(1024)(128)(2,1)}, u32[]{:S(2)}) copy-start(bf16[2048]{0:T(1024)(128)(2,1)} %param.8) | copy-start | bytes 12292
  15.8 5.6 %copy-start.1 = (bf16[2048]{0:T(1024)(128)(2,1)S(1)}, bf16[2048]{0:T(1024)(128)(2,1)}, u32[]{:S(2)}) copy-start(bf16[2048]{0:T(1024)(128)(2,1)} %param.9) | copy-start | bytes 12292
  15.8 31.9 %all-to-all-start = ((bf16[8,64,2048]{2,1,0:T(8,128)(2,1)}), bf16[8,64,2048]{2,1,0:T(8,128)(2,1)S(1)}, u32[]{:S(2)}, u32[]{:S(2)}) async-start(bf16[8,64,2048]{2,1,0:T(8,128)(2,1)} %bitcast.84), calls=%async_computation | async-start | bytes 4194304 | tf_op jit(solution)/shard_map/all_to_all | solution.py:94
  21.2 55.4 %reduce-scatter.3.cloned.1.call-start = ((), (), s32[]{:S(2)}) async-start(), calls=%async_computation.5 | async-start | bytes 716800 | tf_op jit(solution)/shard_map/reduce_scatter | solution.py:123
  54.9 66.1 %reduce-scatter.5.cloned.1.call-start = ((), (), s32[]{:S(2)}) async-start(), calls=%async_computation.6 | async-start | bytes 2621440 | tf_op jit(solution)/shard_map/reduce_scatter | solution.py:129
  66.6 88.0 %all-gather.5.cloned.1.call-start = ((), (), s32[]{:S(2)}) async-start(), calls=%async_computation.7 | async-start | bytes 1310720 | tf_op jit(solution)/shard_map/all_gather | solution.py:149
  127.2 56.4 %all-gather.7.cloned.1.call-start = ((), (), s32[]{:S(2)}) async-start(), calls=%async_computation.8 | async-start | bytes 1310720 | tf_op jit(solution)/shard_map/all_gather | solution.py:149
Sparse Core Ops, SparseCore 0:
  55.1 21.4 reduce-scatter.2
  78.8 42.1 reduce-scatter.4
  127.3 27.2 all-gather.4
  156.1 27.4 all-gather.6
